TPU v7x, 768 devices: a whole 4x8x12 slice. The times are simulated.
768 devices in a mesh: gx: 24 (over y_hi, z), gy: 8 (over y_lo, core), gz: 4 (over x).
Axes of the slice: x: 4, y: 8 (y_hi: 2, y_lo: 4; y = y_hi * 4 + y_lo), z: 12, core: 2. Of those that a mesh axis runs over, the one named last changes fastest.
Arguments:
- state: float32 [5, 192, 64, 512], P(None, 'gx', 'gy', 'gz'), may hold values from -3 to 210, as said below
- register: float32 [5, 192, 64, 512], P(None, 'gx', 'gy', 'gz'), may hold values from -0.5 to 0.5, as said below
Outputs:
- state_next: float32 [5, 192, 64, 512], P(None, 'gx', 'gy', 'gz')
- register_next: float32 [5, 192, 64, 512], P(None, 'gx', 'gy', 'gz')
- coefficients: float32 [2, 192, 64, 512], P(None, 'gx', 'gy', 'gz')
Inputs may be any that keep to these rules, and one draw needn't show every extreme that they name: In every cell the density state[0] lies between 0.125 and 2 and the pressure 0.4 (state[4] - 0.5 (state[1]^2 + state[2]^2 + state[3]^2) / state[0]) is 0.5 or more, up to rounding. The density component register[0] lies within -0.06 and 0.06.
All inputs are finite; a program needn't handle non-finite values.
Results may differ from a plain program's by a relative error of at most 0.00002.
Values sent between devices are 32-bit elements; how exact they have to be, the bound alone decides.
A program may use at most 64 MiB of HBM per device.

v0:
```python
import jax
import jax.numpy as jnp
from jax import lax
from jax.sharding import PartitionSpec as P

LEVELS = 2


WENO_EPS = 1e-06
CFL_NUMBER = 0.3
SECTION_DECAY = -5.0 / 9.0
SECTION_GAIN = 15.0 / 16.0


def extended(block, sides, width):
    for axis, dim in sides:
        count = lax.axis_size(axis)
        forward = [(i, i + 1) for i in range(count - 1)]
        forward.append((count - 1, 0))
        backward = [(target, source) for source, target in forward]
        low = lax.ppermute(
            lax.slice_in_dim(block, block.shape[dim] - width, None, axis=dim), axis, forward
        )
        high = lax.ppermute(lax.slice_in_dim(block, 0, width, axis=dim), axis, backward)
        block = jnp.concatenate([low, block, high], axis=dim)
    return block


def primitives(state):
    density = state[0]
    u = state[1] / density
    v = state[2] / density
    w = state[3] / density
    pressure = 0.4 * (state[4] - 0.5 * density * (u * u + v * v + w * w))
    return jnp.stack([density, u, v, w, pressure])


def weno_face(a, b, c, d, e):
    cand_one = (2.0 * a - 7.0 * b + 11.0 * c) * (1.0 / 6.0)
    cand_two = (-b + 5.0 * c + 2.0 * d) * (1.0 / 6.0)
    cand_three = (2.0 * c + 5.0 * d - e) * (1.0 / 6.0)
    beta_one = 13.0 / 12.0 * jnp.square(a - 2.0 * b + c) + 0.25 * jnp.square(a - 4.0 * b + 3.0 * c)
    beta_two = 13.0 / 12.0 * jnp.square(b - 2.0 * c + d) + 0.25 * jnp.square(b - d)
    beta_three = 13.0 / 12.0 * jnp.square(c - 2.0 * d + e) + 0.25 * jnp.square(
        3.0 * c - 4.0 * d + e
    )
    weight_one = 0.1 / jnp.square(WENO_EPS + beta_one)
    weight_two = 0.6 / jnp.square(WENO_EPS + beta_two)
    weight_three = 0.3 / jnp.square(WENO_EPS + beta_three)
    total = weight_one * cand_one + weight_two * cand_two + weight_three * cand_three
    return total / (weight_one + weight_two + weight_three)


def floor_face(face, lower_cell, upper_cell):
    floor_value = 0.5 * jnp.minimum(lower_cell, upper_cell)
    return jnp.stack(
        [
            jnp.maximum(face[0], floor_value[0]),
            face[1],
            face[2],
            face[3],
            jnp.maximum(face[4], floor_value[4]),
        ]
    )


def state_terms(primitive, dimension):
    density, u, v, w, pressure = (
        primitive[0],
        primitive[1],
        primitive[2],
        primitive[3],
        primitive[4],
    )
    normal = primitive[dimension]
    energy = pressure / 0.4 + 0.5 * density * (u * u + v * v + w * w)
    conserved = jnp.stack([density, density * u, density * v, density * w, energy])
    momentum = [density * u * normal, density * v * normal, density * w * normal]
    momentum[dimension - 1] = momentum[dimension - 1] + pressure
    fluxes = jnp.stack([density * normal] + momentum + [(energy + pressure) * normal])
    sound = jnp.sqrt(1.4 * pressure / density)
    return (conserved, fluxes, normal, sound)


def hlle_flux(left_state, right_state, dimension):
    conserved_left, flux_left, normal_left, sound_left = state_terms(left_state, dimension)
    conserved_right, flux_right, normal_right, sound_right = state_terms(right_state, dimension)
    lower = jnp.minimum(jnp.minimum(normal_left - sound_left, normal_right - sound_right), 0.0)
    upper = jnp.maximum(jnp.maximum(normal_left + sound_left, normal_right + sound_right), 0.0)
    return (
        upper * flux_left - lower * flux_right + upper * lower * (conserved_right - conserved_left)
    ) / (upper - lower)


def face_change(padded, dimension):
    length = padded.shape[dimension] - 6
    shifted = [
        lax.slice_in_dim(padded, index, index + length + 1, 1, dimension) for index in range(6)
    ]
    left_state = floor_face(
        weno_face(shifted[0], shifted[1], shifted[2], shifted[3], shifted[4]),
        shifted[2],
        shifted[3],
    )
    right_state = floor_face(
        weno_face(shifted[5], shifted[4], shifted[3], shifted[2], shifted[1]),
        shifted[2],
        shifted[3],
    )
    fluxes = hlle_flux(left_state, right_state, dimension)
    return lax.slice_in_dim(fluxes, 1, length + 1, 1, dimension) - lax.slice_in_dim(
        fluxes, 0, length, 1, dimension
    )


def pair_up(even_part, odd_part, dimension):
    joined = jnp.stack([even_part, odd_part], axis=dimension + 1)
    new_shape = list(even_part.shape)
    new_shape[dimension] = 2 * new_shape[dimension]
    return joined.reshape(new_shape)


def lift_axis(padded, dimension):
    length = padded.shape[dimension] - 6
    half_length = length // 2
    evens = lax.slice_in_dim(padded, 1, length + 6, 2, dimension)
    odd_part = lax.slice_in_dim(padded, 4, length + 3, 2, dimension)
    even_part = lax.slice_in_dim(evens, 1, half_length + 1, 1, dimension)
    following = lax.slice_in_dim(evens, 2, half_length + 2, 1, dimension)
    previous = lax.slice_in_dim(evens, 0, half_length, 1, dimension)
    further = lax.slice_in_dim(evens, 3, half_length + 3, 1, dimension)
    predicted = (9.0 * (even_part + following) - (previous + further)) * 0.0625
    return pair_up(even_part, odd_part - predicted, dimension)


def local(state, register):
    primitive = primitives(state)
    speed = jnp.maximum(
        jnp.maximum(jnp.abs(primitive[1]), jnp.abs(primitive[2])), jnp.abs(primitive[3])
    ) + jnp.sqrt(1.4 * primitive[4] / primitive[0])
    top_speed = lax.pmax(jnp.max(speed), ("gx", "gy", "gz"))
    step_size = CFL_NUMBER / top_speed
    padded = extended(primitive, (("gx", 1), ("gy", 2), ("gz", 3)), 3)
    change = face_change(padded[:, :, 3:-3, 3:-3], 1)
    change = change + face_change(padded[:, 3:-3, :, 3:-3], 2)
    change = change + face_change(padded[:, 3:-3, 3:-3, :], 3)
    register_next = SECTION_DECAY * register + step_size * -change
    state_next = state + SECTION_GAIN * register_next
    after = primitives(state_next)
    fields = jnp.stack([after[4], after[0]])
    coefficients = fields
    for level_index in range(LEVELS):
        stride = 2**level_index
        coarse = coefficients[:, ::stride, ::stride, ::stride]
        coarse = lift_axis(extended(coarse, (("gx", 1),), 3), 1)
        coarse = lift_axis(extended(coarse, (("gy", 2),), 3), 2)
        coarse = lift_axis(extended(coarse, (("gz", 3),), 3), 3)
        coefficients = coefficients.at[:, ::stride, ::stride, ::stride].set(coarse)
    return (state_next, register_next, coefficients)


def solution(mesh):
    in_specs = (P(None, "gx", "gy", "gz"), P(None, "gx", "gy", "gz"))
    out_specs = (P(None, "gx", "gy", "gz"), P(None, "gx", "gy", "gz"), P(None, "gx", "gy", "gz"))
    return jax.shard_map(local, mesh=mesh, in_specs=in_specs, out_specs=out_specs, check_vma=False)
```

profile of v0, /device:TPU:1, one launch (start us, length us, event | category | flops | bytes accessed | tf_op | source)
XLA Modules:
  0.0 256.0 jit_solution(8002535172028088766)
XLA Ops:
  1.7 4.8 %collective-permute-start = (f32[5,3,8,128]{3,1,2,0:T(4,128)S(1)}, f32[5,3,8,128]{3,1,2,0:T(4,128)S(1)}, u32[]{:S(2)}, u32[]{:S(2)}) collective-permute-start(f32[5,3,8,128]{3,1,2,0:T(4,128)S(1)} %get-tuple-element.122), channel_id=1, source_target_pairs={{0,32},{32,64},{64,96},{96,128},{128,160},{160,192},{192,224},{224... | collective-permute-start | bytes 184328 | tf_op jit(solution)/shard_map/ppermute | solution.py:21
  7.2 17.5 %collective-permute-start.1 = (f32[5,3,8,128]{3,1,2,0:T(4,128)S(1)}, f32[5,3,8,128]{3,1,2,0:T(4,128)S(1)}, u32[]{:S(2)}, u32[]{:S(2)}) collective-permute-start(f32[5,3,8,128]{3,1,2,0:T(4,128)S(1)} %get-tuple-element.123), channel_id=1, source_target_pairs={{32,0},{64,32},{96,64},{128,96},{160,128},{192,160},{224,192},{256... | collective-permute-start | bytes 184328 | tf_op jit(solution)/shard_map/ppermute | solution.py:24
  24.7 105.5 %pmax.7 = f32[]{:T(128)} all-reduce(f32[]{:T(128)} %fusion.114), channel_id=1, replica_groups=mesh['gx'=24,'gy'=8,'gz'=4] {'gx','gy','gz'}, use_global_device_ids=true, to_apply=%region_1.0 | all-reduce | flops 1 | bytes 8 | tf_op jit(solution)/shard_map/pmax | solution.py:141
  131.0 1.9 collective-permute-start.2
  132.9 2.6 %collective-permute-start.3 = (f32[5,14,3,128]{3,1,2,0:T(8,128)S(1)}, f32[5,14,3,128]{3,1,2,0:T(8,128)S(1)}, u32[]{:S(2)}, u32[]{:S(2)}) collective-permute-start(f32[5,14,3,128]{3,1,2,0:T(8,128)S(1)} %get-tuple-element.111), channel_id=1, source_target_pairs={{4,0},{8,4},{12,8},{16,12},{20,16},{24,20},{28,24},{0,28},{5,1},{9... | collective-permute-start | bytes 322568 | tf_op jit(solution)/shard_map/ppermute | solution.py:24
  135.5 1.6 minimum_multiply_fusion.1
  137.7 2.7 %collective-permute-done.3 = f32[5,14,3,128]{3,1,2,0:T(8,128)S(1)} collective-permute-done((f32[5,14,3,128]{3,1,2,0:T(8,128)S(1)}, f32[5,14,3,128]{3,1,2,0:T(8,128)S(1)}, u32[]{:S(2)}, u32[]{:S(2)}) %collective-permute-start.3) | collective-permute-done | bytes 107552 | tf_op jit(solution)/shard_map/ppermute | solution.py:24
  142.0 3.2 %collective-permute-start.5 = (f32[5,14,14,3]{2,1,3,0:T(8,128)S(1)}, f32[5,14,14,3]{2,1,3,0:T(8,128)S(1)}, u32[]{:S(2)}, u32[]{:S(2)}) collective-permute-start(f32[5,14,14,3]{2,1,3,0:T(8,128)S(1)} %copy.83), channel_id=1, source_target_pairs={{1,0},{2,1},{3,2},{0,3},{5,4},{6,5},{7,6},{4,7},{9,8},{10,9},{11,1... | collective-permute-start | bytes 35288 | tf_op jit(solution)/shard_map/ppermute | solution.py:24
  145.1 2.1 collective-permute-start.4
  148.6 3.3 %collective-permute-done.4 = f32[5,14,14,3]{2,1,3,0:T(8,128)S(1)} collective-permute-done((f32[5,14,14,3]{2,1,3,0:T(8,128)S(1)}, f32[5,14,14,3]{2,1,3,0:T(8,128)S(1)}, u32[]{:S(2)}, u32[]{:S(2)}) %collective-permute-start.4) | collective-permute-done | bytes 11792 | tf_op jit(solution)/shard_map/ppermute | solution.py:21
  153.3 1.1 fusion.15
  156.6 3.7 %collective-permute-start.6 = (f32[2,3,8,128]{3,1,2,0:T(4,128)S(1)}, f32[2,3,8,128]{3,1,2,0:T(4,128)S(1)}, u32[]{:S(2)}, u32[]{:S(2)}) collective-permute-start(f32[2,3,8,128]{3,1,2,0:T(4,128)S(1)} %get-tuple-element.134), channel_id=1, source_target_pairs={{0,32},{32,64},{64,96},{96,128},{128,160},{160,192},{192,224},{224... | collective-permute-start | bytes 73736 | tf_op jit(solution)/shard_map/ppermute | solution.py:21
  160.3 7.6 %collective-permute-start.7 = (f32[2,3,8,128]{3,1,2,0:T(4,128)S(1)}, f32[2,3,8,128]{3,1,2,0:T(4,128)S(1)}, u32[]{:S(2)}, u32[]{:S(2)}) collective-permute-start(f32[2,3,8,128]{3,1,2,0:T(4,128)S(1)} %get-tuple-element.135), channel_id=1, source_target_pairs={{32,0},{64,32},{96,64},{128,96},{160,128},{192,160},{224,192},{256... | collective-permute-start | bytes 73736 | tf_op jit(solution)/shard_map/ppermute | solution.py:24
  169.2 4.3 %collective-permute-start.8 = (f32[2,8,3,128]{3,2,1,0:T(4,128)S(1)}, f32[2,8,3,128]{3,2,1,0:T(4,128)S(1)}, u32[]{:S(2)}, u32[]{:S(2)}) collective-permute-start(f32[2,8,3,128]{3,2,1,0:T(4,128)S(1)} %get-tuple-element.130), channel_id=1, source_target_pairs={{0,4},{4,8},{8,12},{12,16},{16,20},{20,24},{24,28},{28,0},{1,5},{5... | collective-permute-start | bytes 73736 | tf_op jit(solution)/shard_map/ppermute | solution.py:21
  173.5 3.2 %collective-permute-start.9 = (f32[2,8,3,128]{3,2,1,0:T(4,128)S(1)}, f32[2,8,3,128]{3,2,1,0:T(4,128)S(1)}, u32[]{:S(2)}, u32[]{:S(2)}) collective-permute-start(f32[2,8,3,128]{3,2,1,0:T(4,128)S(1)} %get-tuple-element.131), channel_id=1, source_target_pairs={{4,0},{8,4},{12,8},{16,12},{20,16},{24,20},{28,24},{0,28},{5,1},{9... | collective-permute-start | bytes 73736 | tf_op jit(solution)/shard_map/ppermute | solution.py:24
  176.8 2.2 collective-permute-done.9
  179.3 1.9 collective-permute-start.10
  181.3 4.8 %collective-permute-start.11 = (f32[2,8,8,3]{3,1,2,0:T(8,128)S(1)}, f32[2,8,8,3]{3,1,2,0:T(8,128)S(1)}, u32[]{:S(2)}, u32[]{:S(2)}) collective-permute-start(f32[2,8,8,3]{3,1,2,0:T(8,128)S(1)} %get-tuple-element.127), channel_id=1, source_target_pairs={{1,0},{2,1},{3,2},{0,3},{5,4},{6,5},{7,6},{4,7},{9,8},{10,9},{11,1... | collective-permute-start | bytes 4616 | tf_op jit(solution)/shard_map/ppermute | solution.py:24
  186.3 1.3 slice.533
  187.7 1.3 slice.531
  189.7 10.7 %slice.537 = f32[2,4,4,64]{2,1,3,0:T(4,128)S(1)} slice(f32[2,8,8,128]{2,1,3,0:T(8,128)S(1)} %bitcast.104), slice={[0:2:1], [0:8:2], [0:8:2], [0:128:2]} | slice | bytes 16384 | tf_op jit(solution)/shard_map/slice | solution.py:154
  200.6 1.9 collective-permute-start.12
  202.5 10.0 %collective-permute-start.13 = (f32[2,3,4,64]{2,1,3,0:T(4,128)S(1)}, f32[2,3,4,64]{2,1,3,0:T(4,128)S(1)}, u32[]{:S(2)}, u32[]{:S(2)}) collective-permute-start(f32[2,3,4,64]{2,1,3,0:T(4,128)S(1)} %get-tuple-element.113), channel_id=1, source_target_pairs={{32,0},{64,32},{96,64},{128,96},{160,128},{192,160},{224,192},{256... | collective-permute-start | bytes 18440 | tf_op jit(solution)/shard_map/ppermute | solution.py:24
  213.5 3.9 %collective-permute-done.12 = f32[2,3,4,64]{2,1,3,0:T(4,128)S(1)} collective-permute-done((f32[2,3,4,64]{2,1,3,0:T(4,128)S(1)}, f32[2,3,4,64]{2,1,3,0:T(4,128)S(1)}, u32[]{:S(2)}, u32[]{:S(2)}) %collective-permute-start.12) | collective-permute-done | bytes 6176 | tf_op jit(solution)/shard_map/ppermute | solution.py:21
  218.9 2.9 %collective-permute-start.14 = (f32[2,4,3,64]{3,2,1,0:T(4,128)S(1)}, f32[2,4,3,64]{3,2,1,0:T(4,128)S(1)}, u32[]{:S(2)}, u32[]{:S(2)}) collective-permute-start(f32[2,4,3,64]{3,2,1,0:T(4,128)S(1)} %get-tuple-element.154), channel_id=1, source_target_pairs={{0,4},{4,8},{8,12},{12,16},{16,20},{20,24},{24,28},{28,0},{1,5},{5... | collective-permute-start | bytes 18440 | tf_op jit(solution)/shard_map/ppermute | solution.py:21
  221.8 6.4 %collective-permute-start.15 = (f32[2,4,3,64]{3,2,1,0:T(4,128)S(1)}, f32[2,4,3,64]{3,2,1,0:T(4,128)S(1)}, u32[]{:S(2)}, u32[]{:S(2)}) collective-permute-start(f32[2,4,3,64]{3,2,1,0:T(4,128)S(1)} %get-tuple-element.155), channel_id=1, source_target_pairs={{4,0},{8,4},{12,8},{16,12},{20,16},{24,20},{28,24},{0,28},{5,1},{9... | collective-permute-start | bytes 18440 | tf_op jit(solution)/shard_map/ppermute | solution.py:24
  229.3 1.9 collective-permute-start.16
  231.2 5.1 %collective-permute-start.17 = (f32[2,4,4,3]{3,2,1,0:T(4,128)S(1)}, f32[2,4,4,3]{3,2,1,0:T(4,128)S(1)}, u32[]{:S(2)}, u32[]{:S(2)}) collective-permute-start(f32[2,4,4,3]{3,2,1,0:T(4,128)S(1)} %get-tuple-element.153), channel_id=1, source_target_pairs={{1,0},{2,1},{3,2},{0,3},{5,4},{6,5},{7,6},{4,7},{9,8},{10,9},{11,1... | collective-permute-start | bytes 1160 | tf_op jit(solution)/shard_map/ppermute | solution.py:24
  237.8 4.5 %copy.88 = f32[2,8,8,64,2]{0,4,3,2,1:T(2,128)} copy(f32[2,8,8,64,2]{3,1,2,0,4:T(8,128)S(1)} %pad_maximum_fusion.22) | data formatting | bytes 131072 | tf_op jit(solution)/shard_map/stack | solution.py:117
  243.4 1.9 copy.99
  245.3 7.2 %scatter_fusion = f32[2,8192]{0,1:T(8,128)} fusion(f32[2,8192]{0,1:T(8,128)} %bitcast.102, s32[1024]{0:T(1024)S(1)} %reshape.70, f32[1024,2]{1,0:T(8,128)S(1)} %bitcast.116), kind=kCustom, calls=%fused_computation | custom fusion | bytes 28672
  252.5 3.5 %copy.98 = f32[2,8,8,128]{3,2,1,0:T(8,128)} copy(f32[2,8,8,128]{0,3,2,1:T(8,128)} %bitcast.103) | data formatting | bytes 131072
  (142 shorter events, 17.1 us)
Async XLA Ops:
  1.7 129.2 %collective-permute-start = (f32[5,3,8,128]{3,1,2,0:T(4,128)S(1)}, f32[5,3,8,128]{3,1,2,0:T(4,128)S(1)}, u32[]{:S(2)}, u32[]{:S(2)}) collective-permute-start(f32[5,3,8,128]{3,1,2,0:T(4,128)S(1)} %get-tuple-element.122), channel_id=1, source_target_pairs={{0,32},{32,64},{64,96},{96,128},{128,160},{160,192},{192,224},{224... | collective-permute-start | bytes 184328 | tf_op jit(solution)/shard_map/ppermute | solution.py:21
  7.2 123.7 %collective-permute-start.1 = (f32[5,3,8,128]{3,1,2,0:T(4,128)S(1)}, f32[5,3,8,128]{3,1,2,0:T(4,128)S(1)}, u32[]{:S(2)}, u32[]{:S(2)}) collective-permute-start(f32[5,3,8,128]{3,1,2,0:T(4,128)S(1)} %get-tuple-element.123), channel_id=1, source_target_pairs={{32,0},{64,32},{96,64},{128,96},{160,128},{192,160},{224,192},{256... | collective-permute-start | bytes 184328 | tf_op jit(solution)/shard_map/ppermute | solution.py:24
  131.0 6.7 %collective-permute-start.2 = (f32[5,14,3,128]{3,1,2,0:T(8,128)S(1)}, f32[5,14,3,128]{3,1,2,0:T(8,128)S(1)}, u32[]{:S(2)}, u32[]{:S(2)}) collective-permute-start(f32[5,14,3,128]{3,1,2,0:T(8,128)S(1)} %get-tuple-element.110), channel_id=1, source_target_pairs={{0,4},{4,8},{8,12},{12,16},{16,20},{20,24},{24,28},{28,0},{1,5},{5... | collective-permute-start | bytes 322568 | tf_op jit(solution)/shard_map/ppermute | solution.py:21
  132.9 7.5 %collective-permute-start.3 = (f32[5,14,3,128]{3,1,2,0:T(8,128)S(1)}, f32[5,14,3,128]{3,1,2,0:T(8,128)S(1)}, u32[]{:S(2)}, u32[]{:S(2)}) collective-permute-start(f32[5,14,3,128]{3,1,2,0:T(8,128)S(1)} %get-tuple-element.111), channel_id=1, source_target_pairs={{4,0},{8,4},{12,8},{16,12},{20,16},{24,20},{28,24},{0,28},{5,1},{9... | collective-permute-start | bytes 322568 | tf_op jit(solution)/shard_map/ppermute | solution.py:24
  142.0 10.7 %collective-permute-start.5 = (f32[5,14,14,3]{2,1,3,0:T(8,128)S(1)}, f32[5,14,14,3]{2,1,3,0:T(8,128)S(1)}, u32[]{:S(2)}, u32[]{:S(2)}) collective-permute-start(f32[5,14,14,3]{2,1,3,0:T(8,128)S(1)} %copy.83), channel_id=1, source_target_pairs={{1,0},{2,1},{3,2},{0,3},{5,4},{6,5},{7,6},{4,7},{9,8},{10,9},{11,1... | collective-permute-start | bytes 35288 | tf_op jit(solution)/shard_map/ppermute | solution.py:24
  145.1 6.8 %collective-permute-start.4 = (f32[5,14,14,3]{2,1,3,0:T(8,128)S(1)}, f32[5,14,14,3]{2,1,3,0:T(8,128)S(1)}, u32[]{:S(2)}, u32[]{:S(2)}) collective-permute-start(f32[5,14,14,3]{2,1,3,0:T(8,128)S(1)} %copy.81), channel_id=1, source_target_pairs={{0,1},{1,2},{2,3},{3,0},{4,5},{5,6},{6,7},{7,4},{8,9},{9,10},{10,1... | collective-permute-start | bytes 35288 | tf_op jit(solution)/shard_map/ppermute | solution.py:21
  155.4 0.9 copy-start
  155.4 1.0 copy-start.1
  156.0 30.2 %copy-start.3 = (s32[3]{0:T(128)S(1)}, s32[3]{0:T(128)}, u32[]{:S(2)}) copy-start(s32[3]{0:T(128)} %constant.70) | copy-start | bytes 40
  156.4 56.1 %copy-start.2 = (s32[3]{0:T(128)S(1)}, s32[3]{0:T(128)}, u32[]{:S(2)}) copy-start(s32[3]{0:T(128)} %constant.67) | copy-start | bytes 40
  156.6 11.4 %collective-permute-start.6 = (f32[2,3,8,128]{3,1,2,0:T(4,128)S(1)}, f32[2,3,8,128]{3,1,2,0:T(4,128)S(1)}, u32[]{:S(2)}, u32[]{:S(2)}) collective-permute-start(f32[2,3,8,128]{3,1,2,0:T(4,128)S(1)} %get-tuple-element.134), channel_id=1, source_target_pairs={{0,32},{32,64},{64,96},{96,128},{128,160},{160,192},{192,224},{224... | collective-permute-start | bytes 73736 | tf_op jit(solution)/shard_map/ppermute | solution.py:21
  160.3 8.7 %collective-permute-start.7 = (f32[2,3,8,128]{3,1,2,0:T(4,128)S(1)}, f32[2,3,8,128]{3,1,2,0:T(4,128)S(1)}, u32[]{:S(2)}, u32[]{:S(2)}) collective-permute-start(f32[2,3,8,128]{3,1,2,0:T(4,128)S(1)} %get-tuple-element.135), channel_id=1, source_target_pairs={{32,0},{64,32},{96,64},{128,96},{160,128},{192,160},{224,192},{256... | collective-permute-start | bytes 73736 | tf_op jit(solution)/shard_map/ppermute | solution.py:24
  169.2 7.7 %collective-permute-start.8 = (f32[2,8,3,128]{3,2,1,0:T(4,128)S(1)}, f32[2,8,3,128]{3,2,1,0:T(4,128)S(1)}, u32[]{:S(2)}, u32[]{:S(2)}) collective-permute-start(f32[2,8,3,128]{3,2,1,0:T(4,128)S(1)} %get-tuple-element.130), channel_id=1, source_target_pairs={{0,4},{4,8},{8,12},{12,16},{16,20},{20,24},{24,28},{28,0},{1,5},{5... | collective-permute-start | bytes 73736 | tf_op jit(solution)/shard_map/ppermute | solution.py:21
  173.5 5.5 %collective-permute-start.9 = (f32[2,8,3,128]{3,2,1,0:T(4,128)S(1)}, f32[2,8,3,128]{3,2,1,0:T(4,128)S(1)}, u32[]{:S(2)}, u32[]{:S(2)}) collective-permute-start(f32[2,8,3,128]{3,2,1,0:T(4,128)S(1)} %get-tuple-element.131), channel_id=1, source_target_pairs={{4,0},{8,4},{12,8},{16,12},{20,16},{24,20},{28,24},{0,28},{5,1},{9... | collective-permute-start | bytes 73736 | tf_op jit(solution)/shard_map/ppermute | solution.py:24
  179.3 8.2 %collective-permute-start.10 = (f32[2,8,8,3]{3,1,2,0:T(8,128)S(1)}, f32[2,8,8,3]{3,1,2,0:T(8,128)S(1)}, u32[]{:S(2)}, u32[]{:S(2)}) collective-permute-start(f32[2,8,8,3]{3,1,2,0:T(8,128)S(1)} %get-tuple-element.126), channel_id=1, source_target_pairs={{0,1},{1,2},{2,3},{3,0},{4,5},{5,6},{6,7},{7,4},{8,9},{9,10},{10,1... | collective-permute-start | bytes 4616 | tf_op jit(solution)/shard_map/ppermute | solution.py:21
  181.3 6.3 %collective-permute-start.11 = (f32[2,8,8,3]{3,1,2,0:T(8,128)S(1)}, f32[2,8,8,3]{3,1,2,0:T(8,128)S(1)}, u32[]{:S(2)}, u32[]{:S(2)}) collective-permute-start(f32[2,8,8,3]{3,1,2,0:T(8,128)S(1)} %get-tuple-element.127), channel_id=1, source_target_pairs={{1,0},{2,1},{3,2},{0,3},{5,4},{6,5},{7,6},{4,7},{9,8},{10,9},{11,1... | collective-permute-start | bytes 4616 | tf_op jit(solution)/shard_map/ppermute | solution.py:24
  200.6 16.8 %collective-permute-start.12 = (f32[2,3,4,64]{2,1,3,0:T(4,128)S(1)}, f32[2,3,4,64]{2,1,3,0:T(4,128)S(1)}, u32[]{:S(2)}, u32[]{:S(2)}) collective-permute-start(f32[2,3,4,64]{2,1,3,0:T(4,128)S(1)} %get-tuple-element.112), channel_id=1, source_target_pairs={{0,32},{32,64},{64,96},{96,128},{128,160},{160,192},{192,224},{224... | collective-permute-start | bytes 18440 | tf_op jit(solution)/shard_map/ppermute | solution.py:21
  202.5 14.9 %collective-permute-start.13 = (f32[2,3,4,64]{2,1,3,0:T(4,128)S(1)}, f32[2,3,4,64]{2,1,3,0:T(4,128)S(1)}, u32[]{:S(2)}, u32[]{:S(2)}) collective-permute-start(f32[2,3,4,64]{2,1,3,0:T(4,128)S(1)} %get-tuple-element.113), channel_id=1, source_target_pairs={{32,0},{64,32},{96,64},{128,96},{160,128},{192,160},{224,192},{256... | collective-permute-start | bytes 18440 | tf_op jit(solution)/shard_map/ppermute | solution.py:24
  218.9 9.4 %collective-permute-start.14 = (f32[2,4,3,64]{3,2,1,0:T(4,128)S(1)}, f32[2,4,3,64]{3,2,1,0:T(4,128)S(1)}, u32[]{:S(2)}, u32[]{:S(2)}) collective-permute-start(f32[2,4,3,64]{3,2,1,0:T(4,128)S(1)} %get-tuple-element.154), channel_id=1, source_target_pairs={{0,4},{4,8},{8,12},{12,16},{16,20},{20,24},{24,28},{28,0},{1,5},{5... | collective-permute-start | bytes 18440 | tf_op jit(solution)/shard_map/ppermute | solution.py:21
  221.8 7.3 %collective-permute-start.15 = (f32[2,4,3,64]{3,2,1,0:T(4,128)S(1)}, f32[2,4,3,64]{3,2,1,0:T(4,128)S(1)}, u32[]{:S(2)}, u32[]{:S(2)}) collective-permute-start(f32[2,4,3,64]{3,2,1,0:T(4,128)S(1)} %get-tuple-element.155), channel_id=1, source_target_pairs={{4,0},{8,4},{12,8},{16,12},{20,16},{24,20},{28,24},{0,28},{5,1},{9... | collective-permute-start | bytes 18440 | tf_op jit(solution)/shard_map/ppermute | solution.py:24
  229.3 13.3 %collective-permute-start.16 = (f32[2,4,4,3]{3,2,1,0:T(4,128)S(1)}, f32[2,4,4,3]{3,2,1,0:T(4,128)S(1)}, u32[]{:S(2)}, u32[]{:S(2)}) collective-permute-start(f32[2,4,4,3]{3,2,1,0:T(4,128)S(1)} %get-tuple-element.152), channel_id=1, source_target_pairs={{0,1},{1,2},{2,3},{3,0},{4,5},{5,6},{6,7},{7,4},{8,9},{9,10},{10,1... | collective-permute-start | bytes 1160 | tf_op jit(solution)/shard_map/ppermute | solution.py:21
  231.2 11.4 %collective-permute-start.17 = (f32[2,4,4,3]{3,2,1,0:T(4,128)S(1)}, f32[2,4,4,3]{3,2,1,0:T(4,128)S(1)}, u32[]{:S(2)}, u32[]{:S(2)}) collective-permute-start(f32[2,4,4,3]{3,2,1,0:T(4,128)S(1)} %get-tuple-element.153), channel_id=1, source_target_pairs={{1,0},{2,1},{3,2},{0,3},{5,4},{6,5},{7,6},{4,7},{9,8},{10,9},{11,1... | collective-permute-start | bytes 1160 | tf_op jit(solution)/shard_map/ppermute | solution.py:24
where the time goes:
time: 260 us; the launch traced here: 256 us
  blocking collectives  106 us (41%)
  starting transfers between devices  85.8 us (33%)
  local copies, waits for them, and re-layouts  40 us (15%)
  waiting for transfers between devices  13.8 us (5%)
  other arithmetic  8.56 us (3%)
    pmax x1, blocking collectives, local(): top_speed = lax.pmax(jnp.max(speed), ('gx', 'gy', 'gz'))  106 us
    ppermute x9, starting transfers between devices, extended(): lax.ppermute(lax.slice_in_dim(block, 0, width, axis=dim), axis, backward)  60.3 us
    ppermute x9, starting transfers between devices, extended(): lax.ppermute(lax.slice_in_dim(block, block.shape[dim] - width, None, axis...  25.5 us
    unnamed x15, local copies, waits for them, and re-layouts  13.2 us
    slice x1, local copies, waits for them, and re-layouts, local(): coarse = coefficients[:, ::stride, ::stride, ::stride]  10.7 us
    ppermute x9, waiting for transfers between devices, extended(): lax.ppermute(lax.slice_in_dim(block, block.shape[dim] - width, None, axis...  7.23 us
    ppermute x9, waiting for transfers between devices, extended(): lax.ppermute(lax.slice_in_dim(block, 0, width, axis=dim), axis, backward)  6.54 us
    another operation x8, local copies, waits for them, and re-layouts, pair_up(): joined = jnp.stack([even_part, odd_part], axis=dimension + 1)  5.43 us
  transfers between devices with their start and end apart: 18, of which 6 were waited for; matrix products, arithmetic and copies ran while one was open for 5% of the time, Pallas kernels for 0%

commit v1 on v0

v1 whole, which is shorter than its diff:
```python
import functools

import jax
import jax.numpy as jnp
from jax import lax
from jax.experimental import pallas as pl
from jax.experimental.pallas import tpu as pltpu
from jax.sharding import PartitionSpec as P

F32 = jnp.float32
CFL_NUMBER = 0.3
SECTION_DECAY = -5.0 / 9.0
SECTION_GAIN = 15.0 / 16.0
NF = 5
LX = 8
LZ = 128
SPARE = (LX + 6) * 8


def weno_pair(a, b, c, d, e):
    e1 = b - a
    e2 = c - b
    e3 = d - c
    e4 = e - d
    d0 = e2 - e1
    d1 = e3 - e2
    d2 = e4 - e3
    g0 = d0 + 2.0 * e2
    g1 = e2 + e3
    g2 = d2 - 2.0 * e3
    third = 13.0 / 3.0
    s0 = (third * d0) * d0 + g0 * g0 + 4e-6
    s1 = (third * d1) * d1 + g1 * g1 + 4e-6
    s2 = (third * d2) * d2 + g2 * g2 + 4e-6
    t0 = s0 * s0
    t1 = s1 * s1
    t2 = s2 * s2
    n0 = t1 * t2
    n1 = 6.0 * (t0 * t2)
    n2 = t0 * t1
    n0_three = 3.0 * n0
    n2_three = 3.0 * n2
    left_up = n0 * (5.0 * e2 - 2.0 * e1) + n1 * (2.0 * e3 + e2) + n2_three * (4.0 * e3 - e4)
    right_up = n2 * (5.0 * e3 - 2.0 * e4) + n1 * (2.0 * e2 + e3) + n0_three * (4.0 * e2 - e1)
    left = c + left_up / (6.0 * (n0 + n1 + n2_three))
    right = c - right_up / (6.0 * (n2 + n1 + n0_three))
    return left, right


def floored(face, lower, upper):
    return (
        jnp.maximum(face[0], 0.5 * jnp.minimum(lower[0], upper[0])),
        face[1],
        face[2],
        face[3],
        jnp.maximum(face[4], 0.5 * jnp.minimum(lower[1], upper[1])),
    )


def hlle(left, right, normal):
    def terms(s):
        rho, u, v, w, p = s
        sound = jnp.sqrt(1.4 * p / rho)
        energy = 2.5 * p + 0.5 * rho * (u * u + v * v + w * w)
        return (rho, rho * u, rho * v, rho * w, energy), s[normal], sound

    ul, nl, cl = terms(left)
    ur, nr, cr = terms(right)
    sm = jnp.minimum(jnp.minimum(nl - cl, nr - cr), 0.0)
    sp = jnp.maximum(jnp.maximum(nl + cl, nr + cr), 0.0)
    inv = 1.0 / (sp - sm)
    spi = sp * inv
    smi = sm * inv
    al = spi * (nl - sm)
    ar = smi * (sp - nr)
    pl_ = spi * left[4]
    pr_ = smi * right[4]
    flux = [al * ul[k] + ar * ur[k] for k in range(NF)]
    flux[normal] = flux[normal] + (pl_ - pr_)
    flux[4] = flux[4] + (pl_ * nl - pr_ * nr)
    return tuple(flux)


def kernel(
    sizes,
    state,
    register,
    o_state,
    o_reg,
    o_coef,
    st,
    rg,
    px,
    py,
    ez,
    ezl,
    ezh,
    ch_x,
    ch_y,
    fz,
    sn,
    rn,
    fe,
    fel,
    feh,
    g0,
    g1,
    mm,
    ml,
    mh,
    sx_hi,
    sx_lo,
    sm_hi,
    sm_lo,
    rx_lo,
    rx_hi,
    cl_lo,
    cl_hi,
    ch_lo,
    ch_hi,
    y0,
    y1,
    mx,
    my,
    mz,
    local_sem,
    halo_send,
    halo_recv,
    max_send,
    max_recv,
    lift_send,
    lift_recv,
):
    nx, ny, nz = sizes
    ix = lax.axis_index("gx")
    iy = lax.axis_index("gy")
    iz = lax.axis_index("gz")

    def at(dx=0, dy=0, dz=0):
        return {
            "gx": lax.rem(ix + (dx + nx), nx),
            "gy": lax.rem(iy + (dy + ny), ny),
            "gz": lax.rem(iz + (dz + nz), nz),
        }

    barrier = pltpu.get_barrier_semaphore()

    def greet(target):
        pl.semaphore_signal(barrier, inc=1, device_id=target, device_id_type=pl.DeviceIdType.MESH)

    load_state = pltpu.make_async_copy(state, st, local_sem.at[0])
    load_reg = pltpu.make_async_copy(register, rg, local_sem.at[1])
    load_state.start()
    load_reg.start()
    for k in range(1, nz):
        greet(at(dz=k))
    for k in range(1, ny):
        greet(at(dy=k))

    def greet_x(k, _):
        greet(at(dx=k))
        return 0

    lax.fori_loop(1, nx, greet_x, 0)
    for dx in (-1, 1):
        for dy in (-1, 1):
            greet(at(dx=dx, dy=dy))
    partners = (nx - 1) + (ny - 1) + (nz - 1) + 4

    lane = lax.broadcasted_iota(jnp.int32, (8, LZ), 1)
    row = lax.broadcasted_iota(jnp.int32, (8, LZ), 0)
    group = lane // 16
    inner = lane % 16

    load_state.wait()

    def make_primitives(x, carry):
        top, edges = carry
        rho = st[0, x]
        inv = 1.0 / rho
        u = st[1, x] * inv
        v = st[2, x] * inv
        w = st[3, x] * inv
        p = 0.4 * (st[4, x] - 0.5 * rho * (u * u + v * v + w * w))
        here = (rho, u, v, w, p)
        rows = pl.ds(pl.multiple_of((x + 3) * 8, 8), 8)
        packed = []
        for k in range(NF):
            px[k, rows, :] = here[k]
            turned = pltpu.roll(here[k], 16 * x + 3, 1)
            packed.append(jnp.where(group == x, turned, edges[k]))
        speed = jnp.maximum(jnp.maximum(jnp.abs(u), jnp.abs(v)), jnp.abs(w)) + jnp.sqrt(1.4 * p * inv)
        return jnp.maximum(top, speed), tuple(packed)

    zero = jnp.zeros((8, LZ), F32)
    top, edges = lax.fori_loop(0, LX, make_primitives, (zero, (zero,) * NF))
    for k in range(NF):
        ez[k] = edges[k]
    top = jnp.max(jnp.max(top, axis=0, keepdims=True), axis=1, keepdims=True)
    mz[0] = jnp.broadcast_to(top, (1, LZ))

    def turn(y, _):
        rows = pl.ds(pl.multiple_of((y + 3) * 8, 8), 8)
        for k in range(NF):
            py[k, rows, :] = px[k, pl.ds(24 + y, 8, stride=8), :]
        return 0

    lax.fori_loop(0, LX, turn, 0)

    pl.semaphore_wait(barrier, partners)

    def remote(src, dst, send, recv, target):
        return pltpu.make_async_remote_copy(
            src_ref=src,
            dst_ref=dst,
            send_sem=send,
            recv_sem=recv,
            device_id=target,
            device_id_type=pl.DeviceIdType.MESH,
        )

    def max_copy(slots, base, k, target):
        return remote(slots.at[0], slots.at[k], max_send.at[base + k], max_recv.at[base + k], target)

    def max_start(slots, count, base, name):
        def body(k, _):
            max_copy(slots, base, k, at(**{name: k})).start()
            return 0

        lax.fori_loop(1, count, body, 0)

    def max_wait(slots, count, base, name):
        def body(k, best):
            max_copy(slots, base, k, at(**{name: k})).wait_recv()
            return jnp.maximum(best, slots[k])

        return lax.fori_loop(1, count, body, slots[0])

    def max_sent(slots, count, base, name):
        def body(k, _):
            max_copy(slots, base, k, at(**{name: k})).wait_send()
            return 0

        lax.fori_loop(1, count, body, 0)

    low, high = pl.ds(0, 24), pl.ds(88, 24)
    first, last = pl.ds(24, 24), pl.ds(64, 24)
    halos = [
        remote(ez, ezl, halo_send.at[0], halo_recv.at[0], at(dz=1)),
        remote(ez, ezh, halo_send.at[1], halo_recv.at[1], at(dz=-1)),
        remote(py.at[:, last, :], py.at[:, low, :], halo_send.at[2], halo_recv.at[2], at(dy=1)),
        remote(py.at[:, first, :], py.at[:, high, :], halo_send.at[3], halo_recv.at[3], at(dy=-1)),
        remote(px.at[:, last, :], px.at[:, low, :], halo_send.at[4], halo_recv.at[4], at(dx=1)),
        remote(px.at[:, first, :], px.at[:, high, :], halo_send.at[5], halo_recv.at[5], at(dx=-1)),
    ]
    max_start(mz, nz, 0, "dz")
    for copy in (halos[4], halos[5], halos[2], halos[3], halos[0], halos[1]):
        copy.start()
    my[0] = max_wait(mz, nz, 0, "dz")
    max_start(my, ny, nz, "dy")

    halos[0].wait_recv()
    halos[1].wait_recv()
    for k in range(NF):
        lower = jnp.where(inner < 3, ezl[k], ez[k])
        upper = pltpu.roll(jnp.where(inner < 3, ez[k], ezh[k]), 8, 1)
        px[k, pl.ds(SPARE, 8), :] = jnp.where(inner < 8, lower, upper)

    def z_faces(x, _):
        rows = pl.ds(pl.multiple_of((x + 3 + 3 * (x // LX)) * 8, 8), 8)
        left, right, cell, nxt = [], [], [], []
        for k in range(NF):
            c = px[k, rows, :]
            outside = pltpu.roll(jnp.where(inner < 3, ezl[k], ezh[k]), lax.rem(253 - 16 * x, LZ), 1)
            a = pltpu.roll(jnp.where(lane >= LZ - 2, outside, c), 2, 1)
            b = pltpu.roll(jnp.where(lane >= LZ - 1, outside, c), 1, 1)
            d = pltpu.roll(jnp.where(lane < 1, outside, c), LZ - 1, 1)
            e = pltpu.roll(jnp.where(lane < 2, outside, c), LZ - 2, 1)
            lk, rk = weno_pair(a, b, c, d, e)
            left.append(lk)
            right.append(pltpu.roll(rk, LZ - 1, 1))
            cell.append(c)
            nxt.append(d)
        sides = (cell[0], cell[4]), (nxt[0], nxt[4])
        flux = hlle(floored(left, *sides), floored(right, *sides), 3)
        out = pl.ds(pl.multiple_of(x * 8, 8), 8)
        for k in range(NF):
            fz[k, out, :] = flux[k]
        return 0

    lax.fori_loop(0, LX + 1, z_faces, 0)
    for k in range(NF):
        ends = fz[k, pl.ds(64, 8), :]
        fz[k, pl.ds(64, 8), :] = jnp.where(inner == 11, pltpu.roll(ends, 9, 1), ends)

    mx[0] = max_wait(my, ny, nz, "dy")
    max_start(mx, nx, nz + ny, "dx")

    def sweep(padded, change, normal):
        def body(j, carry):
            before, flux_before = carry
            left, right = [], []
            lower, upper = [], []
            for k in range(NF):
                a, b, c, d, e = (
                    padded[k, pl.ds(pl.multiple_of((j + i) * 8, 8), 8), :] for i in range(5)
                )
                lk, rk = weno_pair(a, b, c, d, e)
                left.append(lk)
                right.append(rk)
                if k in (0, 4):
                    lower.append(b)
                    upper.append(c)
            sides = tuple(lower), tuple(upper)
            flux = hlle(floored(before, *sides), floored(right, *sides), normal)
            out = pl.ds(pl.multiple_of(j * 8, 8), 8)
            for k in range(NF):
                change[k, out, :] = flux[k] - flux_before[k]
            return tuple(left), flux

        one = jnp.ones((8, LZ), F32)
        lax.fori_loop(0, LX + 2, body, ((one,) * NF, (one,) * NF))

    halos[2].wait_recv()
    halos[3].wait_recv()
    sweep(py, ch_y, 2)
    halos[4].wait_recv()
    halos[5].wait_recv()
    sweep(px, ch_x, 1)

    load_reg.wait()
    fastest = max_wait(mx, nx, nz + ny, "dx")
    step = jnp.broadcast_to(CFL_NUMBER / fastest, (8, LZ))

    def update(x, edges):
        rows_x = pl.ds(pl.multiple_of((x + 2) * 8, 8), 8)
        rows_z = pl.ds(pl.multiple_of(x * 8, 8), 8)
        new = []
        for k in range(NF):
            faces = fz[k, rows_z, :]
            ends = pltpu.roll(fz[k, pl.ds(64, 8), :], 117 - 16 * x, 1)
            upper = jnp.where(lane == LZ - 1, ends, faces)
            lower = jnp.where(lane == 0, ends, pltpu.roll(faces, 1, 1))
            change = ch_x[k, rows_x, :] + ch_y[k, pl.ds(16 + x, 8, stride=8), :]
            change = change + (upper - lower)
            r = SECTION_DECAY * rg[k, x] - step * change
            s = st[k, x] + SECTION_GAIN * r
            rn[k, x] = r
            sn[k, x] = s
            new.append(s)
        rho = new[0]
        square = new[1] * new[1] + new[2] * new[2] + new[3] * new[3]
        p = 0.4 * (new[4] - 0.5 * square / rho)
        packed = []
        for f, value in enumerate((p, rho)):
            g0[f, x] = value
            packed.append(jnp.where(group == x, pltpu.roll(value, 16 * x + 4, 1), edges[f]))
        return tuple(packed)

    edges = lax.fori_loop(0, LX, update, (zero, zero))
    store_state = pltpu.make_async_copy(sn, o_state, local_sem.at[2])
    store_reg = pltpu.make_async_copy(rn, o_reg, local_sem.at[3])
    fe[0] = edges[0]
    fe[1] = edges[1]
    z_copies = [
        remote(fe, fel, lift_send.at[0], lift_recv.at[0], at(dz=1)),
        remote(fe, feh, lift_send.at[1], lift_recv.at[1], at(dz=-1)),
    ]
    for copy in z_copies:
        copy.start()
    store_state.start()
    store_reg.start()
    for copy in z_copies:
        copy.wait_recv()

    odd_lane = lane % 2 == 1
    mid_lane = lane % 4 == 2

    def lift_z(x, _):
        for f in range(2):
            c = g0[f, x]
            out = pltpu.roll(jnp.where(inner < 4, fel[f], feh[f]), lax.rem(252 - 16 * x, LZ), 1)
            up1 = pltpu.roll(jnp.where(lane < 1, out, c), LZ - 1, 1)
            up3 = pltpu.roll(jnp.where(lane < 3, out, c), LZ - 3, 1)
            down1 = pltpu.roll(c, 1, 1)
            down3 = pltpu.roll(jnp.where(lane >= LZ - 3, out, c), 3, 1)
            up2 = pltpu.roll(jnp.where(lane < 2, out, c), LZ - 2, 1)
            up6 = pltpu.roll(jnp.where(lane < 6, out, c), LZ - 6, 1)
            down2 = pltpu.roll(c, 2, 1)
            down6 = pltpu.roll(jnp.where(lane >= LZ - 6, out, c), 6, 1)
            fine = c - (9.0 * (down1 + up1) - (down3 + up3)) * 0.0625
            coarse = c - (9.0 * (down2 + up2) - (down6 + up6)) * 0.0625
            fine = jnp.where(odd_lane, fine, c)
            coarse = jnp.where(mid_lane, coarse, c)
            g0[f, x] = fine
            g1[f, x] = coarse
            merged = jnp.where(row == 1, pltpu.roll(coarse, 1, 0), jnp.where(row == 4, coarse, fine))
            mm[f, x] = merged
        return 0

    lax.fori_loop(0, LX, lift_z, 0)
    for f in range(2):
        for i, (g, x) in enumerate(((g0, 6), (g1, 4))):
            sx_hi[f, i] = g[f, x]
            sm_hi[f, i] = mm[f, x]
        for i, (g, x) in enumerate(((g0, 0), (g0, 2), (g1, 0), (g1, 4))):
            sx_lo[f, i] = g[f, x]
        for i, x in enumerate((0, 2, 4)):
            sm_lo[f, i] = mm[f, x]
    xy_copies = [
        remote(sx_hi, rx_lo, lift_send.at[2], lift_recv.at[2], at(dx=1)),
        remote(sx_lo, rx_hi, lift_send.at[3], lift_recv.at[3], at(dx=-1)),
        remote(mm, ml, lift_send.at[4], lift_recv.at[4], at(dy=1)),
        remote(mm, mh, lift_send.at[5], lift_recv.at[5], at(dy=-1)),
        remote(sm_hi, cl_lo, lift_send.at[6], lift_recv.at[6], at(dx=1, dy=1)),
        remote(sm_hi, cl_hi, lift_send.at[7], lift_recv.at[7], at(dx=1, dy=-1)),
        remote(sm_lo, ch_lo, lift_send.at[8], lift_recv.at[8], at(dx=-1, dy=1)),
        remote(sm_lo, ch_hi, lift_send.at[9], lift_recv.at[9], at(dx=-1, dy=-1)),
    ]
    for copy in xy_copies:
        copy.start()
    for copy in xy_copies:
        copy.wait_recv()

    odd_row = row % 2 == 1
    mid_row = row % 4 == 2

    def fine_y(c, lower, upper):
        up1 = pltpu.roll(jnp.where(row == 0, upper, c), 7, 0)
        up3 = pltpu.roll(jnp.where(row < 3, upper, c), 5, 0)
        down1 = pltpu.roll(c, 1, 0)
        down3 = pltpu.roll(jnp.where(row == 6, lower, c), 3, 0)
        return jnp.where(odd_row, c - (9.0 * (down1 + up1) - (down3 + up3)) * 0.0625, c)

    def coarse_y(c, lower, upper):
        up2 = jnp.where(row == 6, pltpu.roll(upper, 5, 0), pltpu.roll(c, 6, 0))
        up6 = jnp.where(row == 6, pltpu.roll(upper, 2, 0), pltpu.roll(upper, 1, 0))
        down2 = pltpu.roll(c, 2, 0)
        down6 = pltpu.roll(jnp.where(row == 4, lower, c), 6, 0)
        return jnp.where(mid_row, c - (9.0 * (down2 + up2) - (down6 + up6)) * 0.0625, c)

    for f in range(2):

        def lift_y(x, _, f=f):
            y0[f, x + 1] = fine_y(g0[f, x], ml[f, x], mh[f, x])
            return 0

        lax.fori_loop(0, LX, lift_y, 0)

        def lift_y_coarse(i, _, f=f):
            y1[f, i + 1] = coarse_y(g1[f, 2 * i], ml[f, 2 * i], mh[f, 2 * i])
            return 0

        lax.fori_loop(0, LX // 2, lift_y_coarse, 0)
        y0[f, 0] = fine_y(rx_lo[f, 0], cl_lo[f, 0], cl_hi[f, 0])
        y0[f, 9] = fine_y(rx_hi[f, 0], ch_lo[f, 0], ch_hi[f, 0])
        y0[f, 10] = fine_y(rx_hi[f, 1], ch_lo[f, 1], ch_hi[f, 1])
        y1[f, 0] = coarse_y(rx_lo[f, 1], cl_lo[f, 1], cl_hi[f, 1])
        y1[f, 5] = coarse_y(rx_hi[f, 2], ch_lo[f, 0], ch_hi[f, 0])
        y1[f, 6] = coarse_y(rx_hi[f, 3], ch_lo[f, 2], ch_hi[f, 2])

    even = jnp.logical_and(row % 2 == 0, lane % 2 == 0)
    for f in range(2):
        plane = [y0[f, i] for i in range(11)]
        coarse = [y1[f, i] for i in range(7)]
        fine = {-2: plane[0], 8: plane[9], 10: plane[10]}
        for x in range(LX):
            fine[x] = plane[x + 1]
        for x in range(1, LX, 2):
            guess = (9.0 * (fine[x - 1] + fine[x + 1]) - (fine[x - 3] + fine[x + 3])) * 0.0625
            y0[f, x] = fine[x] - guess
        far = {-4: coarse[0], 0: coarse[1], 2: coarse[2], 4: coarse[3], 6: coarse[4], 8: coarse[5], 12: coarse[6]}
        for x in range(0, LX, 2):
            value = far[x]
            if x % 4 == 2:
                value = value - (9.0 * (far[x - 2] + far[x + 2]) - (far[x - 6] + far[x + 6])) * 0.0625
            g1[f, x] = jnp.where(even, value, fine[x])
        for x in range(1, LX, 2):
            g1[f, x] = y0[f, x]
    store_coef = pltpu.make_async_copy(g1, o_coef, local_sem.at[4])
    store_coef.start()

    for copy in halos + z_copies + xy_copies:
        copy.wait_send()
    max_sent(mz, nz, 0, "dz")
    max_sent(my, ny, nz, "dy")
    max_sent(mx, nx, nz + ny, "dx")
    store_state.wait()
    store_reg.wait()
    store_coef.wait()


def solution(mesh):
    sizes = (mesh.shape["gx"], mesh.shape["gy"], mesh.shape["gz"])
    spec = P(None, "gx", "gy", "gz")
    any_space = pl.BlockSpec(memory_space=pl.ANY)

    def vmem(*shape):
        return pltpu.VMEM(shape, F32)

    plane = (8, LZ)
    total = sum(sizes)
    scratch = [
        vmem(NF, LX, *plane),
        vmem(NF, LX, *plane),
        vmem(NF, SPARE + 8, LZ),
        vmem(NF, SPARE, LZ),
        vmem(NF, *plane),
        vmem(NF, *plane),
        vmem(NF, *plane),
        vmem(NF, (LX + 2) * 8, LZ),
        vmem(NF, (LX + 2) * 8, LZ),
        vmem(NF, (LX + 1) * 8, LZ),
        vmem(NF, LX, *plane),
        vmem(NF, LX, *plane),
        vmem(2, *plane),
        vmem(2, *plane),
        vmem(2, *plane),
        vmem(2, LX, *plane),
        vmem(2, LX, *plane),
        vmem(2, LX, *plane),
        vmem(2, LX, *plane),
        vmem(2, LX, *plane),
        vmem(2, 2, *plane),
        vmem(2, 4, *plane),
        vmem(2, 2, *plane),
        vmem(2, 3, *plane),
        vmem(2, 2, *plane),
        vmem(2, 4, *plane),
        vmem(2, 2, *plane),
        vmem(2, 2, *plane),
        vmem(2, 3, *plane),
        vmem(2, 3, *plane),
        vmem(2, 11, *plane),
        vmem(2, 7, *plane),
        vmem(sizes[0], 1, LZ),
        vmem(sizes[1], 1, LZ),
        vmem(sizes[2], 1, LZ),
        pltpu.SemaphoreType.DMA((5,)),
        pltpu.SemaphoreType.DMA((6,)),
        pltpu.SemaphoreType.DMA((6,)),
        pltpu.SemaphoreType.DMA((total,)),
        pltpu.SemaphoreType.DMA((total,)),
        pltpu.SemaphoreType.DMA((10,)),
        pltpu.SemaphoreType.DMA((10,)),
    ]

    def local(state, register):
        block = jax.ShapeDtypeStruct(state.shape, F32)
        return pl.pallas_call(
            functools.partial(kernel, sizes),
            out_shape=(block, block, jax.ShapeDtypeStruct((2,) + state.shape[1:], F32)),
            in_specs=[any_space] * 2,
            out_specs=(any_space,) * 3,
            scratch_shapes=scratch,
            compiler_params=pltpu.CompilerParams(
                collective_id=0, has_side_effects=True, vmem_limit_bytes=32 * 1024 * 1024
            ),
        )(state, register)

    return jax.shard_map(local, mesh=mesh, in_specs=(spec, spec), out_specs=(spec,) * 3, check_vma=False)
```

time: 260 us -> 56.3 us (0.22); the launches traced: 256 us -> 56.1 us
  blocking collectives: 106 us -> 0 us
  starting transfers between devices: 85.8 us -> 0 us
  Pallas kernels: 0 us -> 51.7 us
  local copies, waits for them, and re-layouts: 40 us -> 3.79 us
  waiting for transfers between devices: 13.8 us -> 0 us
  other arithmetic: 8.56 us -> 0 us
    pmax x1 -> x0, blocking collectives: 106 us -> none  [local(): top_speed = lax.pmax(jnp.max(speed), ('gx', 'gy', 'gz'))]
    ppermute x18 -> x0, starting transfers between devices: 85.8 us -> none  [the longest x9 60.3 us: extended(): lax.ppermute(lax.slice_in_dim(block, 0, width, axis=dim), axis, backward)]
    pallas_call x0 -> x1, Pallas kernels: none -> 51.7 us  [local(): pl.pallas_call(functools.partial(kernel, sizes), out_shape=(block, block,...]
    slice x22 -> x0, local copies, waits for them, and re-layouts: 18 us -> none  [the longest x1 10.7 us: local(): coarse = coefficients[:, ::stride, ::stride, ::stride]]
    ppermute x18 -> x0, waiting for transfers between devices: 13.8 us -> none  [the longest x9 7.23 us: extended(): lax.ppermute(lax.slice_in_dim(block, block.shape[dim] - width, None, axis...]
    unnamed x15 -> x7, local copies, waits for them, and re-layouts: 13.2 us -> 3.79 us
    another operation x14 -> x0, local copies, waits for them, and re-layouts: 5.47 us -> none  [the longest x8 5.43 us: pair_up(): joined = jnp.stack([even_part, odd_part], axis=dimension + 1)]
    mul x9 -> x0, other arithmetic: 3.07 us -> none  [the longest x3 2.81 us: floor_face(): floor_value = 0.5 * jnp.minimum(lower_cell, upper_cell)]
  transfers between devices with their start and end apart: 18 -> 0, of which waited for: 6 -> 0; matrix products, arithmetic and copies ran while one was open for 5% -> 0% of each run, Pallas kernels for 0% -> 0%
where the time goes in v1:
time: 56.3 us; the launch traced here: 56.1 us
  Pallas kernels  51.7 us (92%)
  local copies, waits for them, and re-layouts  3.79 us (7%)
  between operations  0.65 us (1%)
    pallas_call x1, Pallas kernels, local(): pl.pallas_call(functools.partial(kernel, sizes), out_shape=(block, block,...  51.7 us
    unnamed x7, local copies, waits for them, and re-layouts  3.79 us

profile of v1, /device:TPU:1, one launch (start us, length us, event | category | flops | bytes accessed | tf_op | source)
XLA Modules:
  0.0 56.1 jit_solution(11864486817571280311)
XLA Ops:
  0.6 0.0 copy-start
  0.6 0.9 %copy-done = f32[5,8,8,128]{3,2,1,0:T(8,128)S(1)} copy-done((f32[5,8,8,128]{3,2,1,0:T(8,128)S(1)}, f32[5,8,8,128]{3,2,1,0:T(8,128)}, u32[]{:S(2)}) %copy-start) | copy-done | bytes 163864
  1.5 0.0 copy-start.1
  1.5 0.9 %copy-done.1 = f32[5,8,8,128]{3,2,1,0:T(8,128)S(1)} copy-done((f32[5,8,8,128]{3,2,1,0:T(8,128)S(1)}, f32[5,8,8,128]{3,2,1,0:T(8,128)}, u32[]{:S(2)}) %copy-start.1) | copy-done | bytes 163864
  2.5 51.7 %shard_map.49 = (f32[5,8,8,128]{3,2,1,0:T(8,128)S(1)}, f32[5,8,8,128]{3,2,1,0:T(8,128)S(1)}, f32[2,8,8,128]{3,2,1,0:T(8,128)S(1)}) custom-call(f32[5,8,8,128]{3,2,1,0:T(8,128)S(1)} %copy-done, f32[5,8,8,128]{3,2,1,0:T(8,128)S(1)} %copy-done.1), custom_call_target="tpu_custom_call" | custom-call | tf_op jit(solution)/shard_map/pallas_call | solution.py:550
  54.1 0.7 %copy.8 = f32[5,8,8,128]{3,2,1,0:T(8,128)} copy(f32[5,8,8,128]{3,2,1,0:T(8,128)S(1)} %get-tuple-element.6) | data formatting | bytes 327680
  54.8 0.7 %copy.9 = f32[5,8,8,128]{3,2,1,0:T(8,128)} copy(f32[5,8,8,128]{3,2,1,0:T(8,128)S(1)} %get-tuple-element.7) | data formatting | bytes 327680
  55.5 0.6 %copy.10 = f32[2,8,8,128]{3,2,1,0:T(8,128)} copy(f32[2,8,8,128]{3,2,1,0:T(8,128)S(1)} %get-tuple-element.8) | data formatting | bytes 131072
Async XLA Ops:
  0.6 0.9 %copy-start = (f32[5,8,8,128]{3,2,1,0:T(8,128)S(1)}, f32[5,8,8,128]{3,2,1,0:T(8,128)}, u32[]{:S(2)}) copy-start(f32[5,8,8,128]{3,2,1,0:T(8,128)} %state.1) | copy-start | bytes 491524
  1.5 0.9 %copy-start.1 = (f32[5,8,8,128]{3,2,1,0:T(8,128)S(1)}, f32[5,8,8,128]{3,2,1,0:T(8,128)}, u32[]{:S(2)}) copy-start(f32[5,8,8,128]{3,2,1,0:T(8,128)} %register.1) | copy-start | bytes 491524

commit v2 on v1

v2 whole, which is shorter than its diff:
```python
import functools

import jax
import jax.numpy as jnp
from jax import lax
from jax.experimental import pallas as pl
from jax.experimental.pallas import tpu as pltpu
from jax.sharding import PartitionSpec as P

F32 = jnp.float32
CFL_NUMBER = 0.3
SECTION_DECAY = -5.0 / 9.0
SECTION_GAIN = 15.0 / 16.0
NF = 5
LX = 8
LZ = 128
SPARE = (LX + 6) * 8


def weno_pair(a, b, c, d, e):
    e1 = b - a
    e2 = c - b
    e3 = d - c
    e4 = e - d
    d0 = e2 - e1
    d1 = e3 - e2
    d2 = e4 - e3
    g0 = d0 + 2.0 * e2
    g1 = e2 + e3
    g2 = d2 - 2.0 * e3
    third = 13.0 / 3.0
    s0 = (third * d0) * d0 + g0 * g0 + 4e-6
    s1 = (third * d1) * d1 + g1 * g1 + 4e-6
    s2 = (third * d2) * d2 + g2 * g2 + 4e-6
    t0 = s0 * s0
    t1 = s1 * s1
    t2 = s2 * s2
    n0 = t1 * t2
    n1 = 6.0 * (t0 * t2)
    n2 = t0 * t1
    n0_three = 3.0 * n0
    n2_three = 3.0 * n2
    left_up = n0 * (5.0 * e2 - 2.0 * e1) + n1 * (2.0 * e3 + e2) + n2_three * (4.0 * e3 - e4)
    right_up = n2 * (5.0 * e3 - 2.0 * e4) + n1 * (2.0 * e2 + e3) + n0_three * (4.0 * e2 - e1)
    left = c + left_up / (6.0 * (n0 + n1 + n2_three))
    right = c - right_up / (6.0 * (n2 + n1 + n0_three))
    return left, right


def floored(face, lower, upper):
    return (
        jnp.maximum(face[0], 0.5 * jnp.minimum(lower[0], upper[0])),
        face[1],
        face[2],
        face[3],
        jnp.maximum(face[4], 0.5 * jnp.minimum(lower[1], upper[1])),
    )


def hlle(left, right, normal):
    def terms(s):
        rho, u, v, w, p = s
        sound = jnp.sqrt(1.4 * p / rho)
        energy = 2.5 * p + 0.5 * rho * (u * u + v * v + w * w)
        return (rho, rho * u, rho * v, rho * w, energy), s[normal], sound

    ul, nl, cl = terms(left)
    ur, nr, cr = terms(right)
    sm = jnp.minimum(jnp.minimum(nl - cl, nr - cr), 0.0)
    sp = jnp.maximum(jnp.maximum(nl + cl, nr + cr), 0.0)
    inv = 1.0 / (sp - sm)
    spi = sp * inv
    smi = sm * inv
    al = spi * (nl - sm)
    ar = smi * (sp - nr)
    pl_ = spi * left[4]
    pr_ = smi * right[4]
    flux = [al * ul[k] + ar * ur[k] for k in range(NF)]
    flux[normal] = flux[normal] + (pl_ - pr_)
    flux[4] = flux[4] + (pl_ * nl - pr_ * nr)
    return tuple(flux)


def kernel(
    sizes,
    state,
    register,
    o_state,
    o_reg,
    o_coef,
    st,
    rg,
    px,
    py,
    ez,
    ezl,
    ezh,
    ch_x,
    ch_y,
    fz,
    sn,
    rn,
    en,
    ey,
    turned,
    around,
    sx_hi,
    sx_lo,
    rx_lo,
    rx_hi,
    sz,
    rz_lo,
    rz_hi,
    fn,
    fy,
    fc,
    coef,
    mx,
    my,
    mz,
    local_sem,
    halo_send,
    halo_recv,
    max_send,
    max_recv,
    lift_send,
    lift_recv,
):
    nx, ny, nz = sizes
    ix = lax.axis_index("gx")
    iy = lax.axis_index("gy")
    iz = lax.axis_index("gz")

    def at(dx=0, dy=0, dz=0):
        return {
            "gx": lax.rem(ix + (dx + nx), nx),
            "gy": lax.rem(iy + (dy + ny), ny),
            "gz": lax.rem(iz + (dz + nz), nz),
        }

    chips_z, half_y = nx // 2, ny // 2

    def plane_mate(k):
        return {"gx": ix, "gy": iy - iy % 2 + (iy + k // nz) % 2, "gz": (iz + k % nz) % nz}

    def column_mate(k):
        y = (ix // chips_z * half_y + iy // 2 + k) % (2 * half_y)
        return {"gx": y // half_y * chips_z + ix % chips_z, "gy": y % half_y * 2 + iy % 2, "gz": iz}

    def depth_mate(k):
        return {"gx": ix - ix % chips_z + (ix + k) % chips_z, "gy": iy, "gz": iz}

    groups = ((plane_mate, 2 * nz), (column_mate, 2 * half_y), (depth_mate, chips_z))

    barrier = pltpu.get_barrier_semaphore()

    def greet(target):
        pl.semaphore_signal(barrier, inc=1, device_id=target, device_id_type=pl.DeviceIdType.MESH)

    load_state = pltpu.make_async_copy(state, st, local_sem.at[0])
    load_reg = pltpu.make_async_copy(register, rg, local_sem.at[1])
    load_state.start()
    load_reg.start()
    for mate, count in groups:

        def greet_mate(k, _, mate=mate):
            greet(mate(k))
            return 0

        lax.fori_loop(1, count, greet_mate, 0)
    for target in (at(dx=-1), at(dx=1), at(dy=-1), at(dy=1), at(dz=-1), at(dz=1)):
        greet(target)
    partners = sum(count - 1 for _, count in groups) + 6

    lane = lax.broadcasted_iota(jnp.int32, (8, LZ), 1)
    row = lax.broadcasted_iota(jnp.int32, (8, LZ), 0)
    group = lane // 16
    inner = lane % 16

    load_state.wait()

    def make_primitives(x, top):
        rho = st[0, x]
        inv = 1.0 / rho
        u = st[1, x] * inv
        v = st[2, x] * inv
        w = st[3, x] * inv
        p = 0.4 * (st[4, x] - 0.5 * rho * (u * u + v * v + w * w))
        here = (rho, u, v, w, p)
        rows = pl.ds(pl.multiple_of((x + 3) * 8, 8), 8)
        for k in range(NF):
            px[k, rows, :] = here[k]
        speed = jnp.maximum(jnp.maximum(jnp.abs(u), jnp.abs(v)), jnp.abs(w)) + jnp.sqrt(1.4 * p * inv)
        return jnp.maximum(top, speed)

    zero = jnp.zeros((8, LZ), F32)
    top = lax.fori_loop(0, LX, make_primitives, zero)
    top = jnp.max(jnp.max(top, axis=0, keepdims=True), axis=1, keepdims=True)
    mz[0] = jnp.broadcast_to(top, (1, LZ))

    pl.semaphore_wait(barrier, partners)

    def remote(src, dst, send, recv, target):
        return pltpu.make_async_remote_copy(
            src_ref=src,
            dst_ref=dst,
            send_sem=send,
            recv_sem=recv,
            device_id=target,
            device_id_type=pl.DeviceIdType.MESH,
        )

    bases = (0, groups[0][1], groups[0][1] + groups[1][1])
    slots = (mz, my, mx)

    def max_copy(i, k):
        base = bases[i]
        return remote(slots[i].at[0], slots[i].at[k], max_send.at[base + k], max_recv.at[base + k], groups[i][0](k))

    def max_start(i):
        def body(k, _):
            max_copy(i, k).start()
            return 0

        lax.fori_loop(1, groups[i][1], body, 0)

    def max_wait(i):
        def body(k, best):
            max_copy(i, k).wait_recv()
            return jnp.maximum(best, slots[i][k])

        return lax.fori_loop(1, groups[i][1], body, slots[i][0])

    def max_sent(i):
        def body(k, _):
            max_copy(i, k).wait_send()
            return 0

        lax.fori_loop(1, groups[i][1], body, 0)

    max_start(0)

    low, high = pl.ds(0, 24), pl.ds(88, 24)
    first, last = pl.ds(24, 24), pl.ds(64, 24)
    halos = [
        remote(ez, ezl, halo_send.at[0], halo_recv.at[0], at(dz=1)),
        remote(ez, ezh, halo_send.at[1], halo_recv.at[1], at(dz=-1)),
        remote(py.at[:, last, :], py.at[:, low, :], halo_send.at[2], halo_recv.at[2], at(dy=1)),
        remote(py.at[:, first, :], py.at[:, high, :], halo_send.at[3], halo_recv.at[3], at(dy=-1)),
        remote(px.at[:, last, :], px.at[:, low, :], halo_send.at[4], halo_recv.at[4], at(dx=1)),
        remote(px.at[:, first, :], px.at[:, high, :], halo_send.at[5], halo_recv.at[5], at(dx=-1)),
    ]
    halos[4].start()
    halos[5].start()

    def turn(y, _):
        rows = pl.ds(pl.multiple_of((y + 3) * 8, 8), 8)
        for k in range(NF):
            py[k, rows, :] = px[k, pl.ds(24 + y, 8, stride=8), :]
        return 0

    lax.fori_loop(0, LX, turn, 0)
    halos[2].start()
    halos[3].start()

    def pack_edges(x, edges):
        rows = pl.ds(pl.multiple_of((x + 3) * 8, 8), 8)
        return tuple(
            jnp.where(group == x, pltpu.roll(px[k, rows, :], 16 * x + 3, 1), edges[k]) for k in range(NF)
        )

    edges = lax.fori_loop(0, LX, pack_edges, (zero,) * NF)
    for k in range(NF):
        ez[k] = edges[k]
    halos[0].start()
    halos[1].start()

    def slot(i):
        return pl.ds(8 * i if isinstance(i, int) else pl.multiple_of(i * 8, 8), 8)

    def lift_copies(v):
        def one(i, src, dst, target):
            return remote(src, dst, lift_send.at[4 * v + i], lift_recv.at[4 * v + i], target)

        to_hi, to_lo = pl.ds(0, 16), pl.ds(16, 24)
        return [
            one(0, turned.at[v, :, to_hi, :], around.at[v, :, to_hi, :], at(dy=1)),
            one(1, turned.at[v, :, to_lo, :], around.at[v, :, to_lo, :], at(dy=-1)),
            one(2, sz.at[v], rz_lo.at[v], at(dz=1)),
            one(3, sz.at[v], rz_hi.at[v], at(dz=-1)),
        ]

    lifts = [lift_copies(0), lift_copies(1)]
    for v in range(2):
        for k in range(NF):
            around[v, k, pl.ds(40, 24), :] = jnp.zeros((24, LZ), F32)

    def send_rows(v):
        for k in range(NF):
            for i, y in enumerate((4, 6, 0, 2, 4)):
                turned[v, k, pl.ds(8 * i, 8), :] = en[v, k, pl.ds(y, 8, stride=8), :]
        lifts[v][0].start()
        lifts[v][1].start()

    def send_ends(v):
        lifts[v][0].wait_recv()
        lifts[v][1].wait_recv()

        def pack_ends(x, packed):
            out = []
            for k in range(NF):
                outer = around[v, k, pl.ds(x, 8, stride=8), :]
                ey[v, k, slot(x), :] = outer
                for j, value in enumerate((en[v, k, slot(x), :], outer)):
                    out.append(jnp.where(group == x, pltpu.roll(value, 16 * x + 4, 1), packed[2 * k + j]))
            return tuple(out)

        packed = lax.fori_loop(0, LX, pack_ends, (zero,) * (2 * NF))
        for k in range(NF):
            sz[v, k, pl.ds(0, 8), :] = packed[2 * k]
            sz[v, k, pl.ds(8, 8), :] = packed[2 * k + 1]
        lifts[v][2].start()
        lifts[v][3].start()

    load_reg.wait()

    def make_base(x, _):
        for k in range(NF):
            en[0, k, slot(x), :] = st[k, x] + (SECTION_GAIN * SECTION_DECAY) * rg[k, x]
        return 0

    lax.fori_loop(0, LX, make_base, 0)
    send_rows(0)

    my[0] = max_wait(0)
    max_start(1)

    halos[0].wait_recv()
    halos[1].wait_recv()
    for k in range(NF):
        lower = jnp.where(inner < 3, ezl[k], ez[k])
        upper = pltpu.roll(jnp.where(inner < 3, ez[k], ezh[k]), 8, 1)
        px[k, pl.ds(SPARE, 8), :] = jnp.where(inner < 8, lower, upper)

    def z_faces(x, _):
        rows = pl.ds(pl.multiple_of((x + 3 + 3 * (x // LX)) * 8, 8), 8)
        left, right, cell, nxt = [], [], [], []
        for k in range(NF):
            c = px[k, rows, :]
            outside = pltpu.roll(jnp.where(inner < 3, ezl[k], ezh[k]), lax.rem(253 - 16 * x, LZ), 1)
            a = pltpu.roll(jnp.where(lane >= LZ - 2, outside, c), 2, 1)
            b = pltpu.roll(jnp.where(lane >= LZ - 1, outside, c), 1, 1)
            d = pltpu.roll(jnp.where(lane < 1, outside, c), LZ - 1, 1)
            e = pltpu.roll(jnp.where(lane < 2, outside, c), LZ - 2, 1)
            lk, rk = weno_pair(a, b, c, d, e)
            left.append(lk)
            right.append(pltpu.roll(rk, LZ - 1, 1))
            cell.append(c)
            nxt.append(d)
        sides = (cell[0], cell[4]), (nxt[0], nxt[4])
        flux = hlle(floored(left, *sides), floored(right, *sides), 3)
        out = pl.ds(pl.multiple_of(x * 8, 8), 8)
        for k in range(NF):
            fz[k, out, :] = flux[k]
        return 0

    lax.fori_loop(0, LX + 1, z_faces, 0)
    for k in range(NF):
        ends = fz[k, pl.ds(64, 8), :]
        fz[k, pl.ds(64, 8), :] = jnp.where(inner == 11, pltpu.roll(ends, 9, 1), ends)

    def sweep(padded, change, normal):
        def body(j, carry):
            before, flux_before = carry
            left, right = [], []
            lower, upper = [], []
            for k in range(NF):
                a, b, c, d, e = (
                    padded[k, pl.ds(pl.multiple_of((j + i) * 8, 8), 8), :] for i in range(5)
                )
                lk, rk = weno_pair(a, b, c, d, e)
                left.append(lk)
                right.append(rk)
                if k in (0, 4):
                    lower.append(b)
                    upper.append(c)
            sides = tuple(lower), tuple(upper)
            flux = hlle(floored(before, *sides), floored(right, *sides), normal)
            out = pl.ds(pl.multiple_of(j * 8, 8), 8)
            for k in range(NF):
                change[k, out, :] = flux[k] - flux_before[k]
            return tuple(left), flux

        one = jnp.ones((8, LZ), F32)
        lax.fori_loop(0, LX + 2, body, ((one,) * NF, (one,) * NF))

    halos[2].wait_recv()
    halos[3].wait_recv()
    sweep(py, ch_y, 2)
    send_ends(0)
    mx[0] = max_wait(1)
    max_start(2)
    halos[4].wait_recv()
    halos[5].wait_recv()
    sweep(px, ch_x, 1)

    def make_rate(x, _):
        rows_x = slot(x + 2)
        rows_z = slot(x)
        for k in range(NF):
            faces = fz[k, rows_z, :]
            ends = pltpu.roll(fz[k, pl.ds(64, 8), :], 117 - 16 * x, 1)
            upper = jnp.where(lane == LZ - 1, ends, faces)
            lower = jnp.where(lane == 0, ends, pltpu.roll(faces, 1, 1))
            change = ch_x[k, rows_x, :] + ch_y[k, pl.ds(16 + x, 8, stride=8), :]
            en[1, k, rows_z, :] = -(change + (upper - lower))
        return 0

    lax.fori_loop(0, LX, make_rate, 0)
    send_rows(1)
    send_ends(1)
    for v in range(2):
        lifts[v][2].wait_recv()
        lifts[v][3].wait_recv()

    fastest = max_wait(2)
    step = jnp.broadcast_to(CFL_NUMBER / fastest, (8, LZ))
    gain = SECTION_GAIN * step

    def pressure(new):
        square = new[1] * new[1] + new[2] * new[2] + new[3] * new[3]
        return 0.4 * (new[4] - 0.5 * square / new[0])

    from_low = inner < 4
    for j in range(2):
        rows = pl.ds(8 * j, 8)
        new = []
        for k in range(NF):
            base = jnp.where(from_low, rz_lo[0, k, rows, :], rz_hi[0, k, rows, :])
            rate = jnp.where(from_low, rz_lo[1, k, rows, :], rz_hi[1, k, rows, :])
            new.append(base + gain * rate)
        fc[0, rows, :] = pressure(new)
        fc[1, rows, :] = new[0]

    def after(ref, x):
        new = [ref[0, k, slot(x), :] + gain * ref[1, k, slot(x), :] for k in range(NF)]
        return pressure(new), new[0]

    odd_lane = lane % 2 == 1
    mid_lane = lane % 4 == 2
    odd_row = row % 2 == 1
    mid_row = row % 4 == 2

    def predicted(down1, up1, down3, up3):
        return (9.0 * (down1 + up1) - (down3 + up3)) * 0.0625

    def fine_z(c, ends):
        up1 = pltpu.roll(jnp.where(lane < 1, ends, c), LZ - 1, 1)
        up3 = pltpu.roll(jnp.where(lane < 3, ends, c), LZ - 3, 1)
        down1 = pltpu.roll(c, 1, 1)
        down3 = pltpu.roll(jnp.where(lane >= LZ - 3, ends, c), 3, 1)
        return jnp.where(odd_lane, c - predicted(down1, up1, down3, up3), c)

    def coarse_z(c, ends):
        up2 = pltpu.roll(jnp.where(lane < 2, ends, c), LZ - 2, 1)
        up6 = pltpu.roll(jnp.where(lane < 6, ends, c), LZ - 6, 1)
        down2 = pltpu.roll(c, 2, 1)
        down6 = pltpu.roll(jnp.where(lane >= LZ - 6, ends, c), 6, 1)
        return jnp.where(mid_lane, c - predicted(down2, up2, down6, up6), c)

    def fine_y(c, outer):
        down1 = pltpu.roll(c, 1, 0)
        down3 = jnp.where(row == 1, outer, pltpu.roll(c, 3, 0))
        up1 = jnp.where(row == 7, pltpu.roll(outer, 5, 0), pltpu.roll(c, 7, 0))
        up3 = jnp.where(row == 7, pltpu.roll(outer, 4, 0), pltpu.roll(c, 5, 0))
        up3 = jnp.where(row == 5, pltpu.roll(outer, 3, 0), up3)
        return jnp.where(odd_row, c - predicted(down1, up1, down3, up3), c)

    def coarse_y(c, outer):
        down2 = pltpu.roll(c, 2, 0)
        further = pltpu.roll(c, 6, 0)
        beyond = pltpu.roll(outer, 2, 0)
        up2 = jnp.where(row == 6, pltpu.roll(outer, 4, 0), further)
        down6 = jnp.where(row == 2, beyond, further)
        up6 = jnp.where(row == 2, outer, beyond)
        return jnp.where(mid_row, c - predicted(down2, up2, down6, up6), c)

    def lift_zy(x, both):
        shift = lax.rem(252 - 16 * x, LZ)
        cells, outer = after(en, x), after(ey, x)
        for f in range(2):
            ends = pltpu.roll(fc[f, pl.ds(0, 8), :], shift, 1)
            ends_outer = pltpu.roll(fc[f, pl.ds(8, 8), :], shift, 1)
            fn[f, slot(x), :] = fine_y(fine_z(cells[f], ends), fine_z(outer[f], ends_outer))
            if both:
                fy[f, slot(x), :] = coarse_y(coarse_z(cells[f], ends), coarse_z(outer[f], ends_outer))

    def lift_even(i, _):
        lift_zy(2 * i, True)
        return 0

    lax.fori_loop(0, LX // 2, lift_even, 0)

    for f in range(2):
        sx_hi[f, slot(0), :] = fn[f, slot(6), :]
        sx_hi[f, slot(1), :] = fy[f, slot(4), :]
        sx_lo[f, slot(0), :] = fn[f, slot(0), :]
        sx_lo[f, slot(1), :] = fn[f, slot(2), :]
        sx_lo[f, slot(2), :] = jnp.where(odd_row, pltpu.roll(fy[f, slot(4), :], 1, 0), fy[f, slot(0), :])
    x_copies = [
        remote(sx_hi, rx_lo, lift_send.at[8], lift_recv.at[8], at(dx=1)),
        remote(sx_lo, rx_hi, lift_send.at[9], lift_recv.at[9], at(dx=-1)),
    ]
    for copy in x_copies:
        copy.start()

    def update(x, _):
        for k in range(NF):
            r = SECTION_DECAY * rg[k, x] + step * en[1, k, slot(x), :]
            rn[k, x] = r
            sn[k, x] = st[k, x] + SECTION_GAIN * r
        return 0

    lax.fori_loop(0, LX, update, 0)
    store_state = pltpu.make_async_copy(sn, o_state, local_sem.at[2])
    store_reg = pltpu.make_async_copy(rn, o_reg, local_sem.at[3])
    store_state.start()
    store_reg.start()

    def lift_odd(i, _):
        lift_zy(2 * i + 1, False)
        return 0

    lax.fori_loop(0, LX // 2, lift_odd, 0)

    for copy in x_copies:
        copy.wait_recv()
    even = jnp.logical_and(row % 2 == 0, lane % 2 == 0)
    for f in range(2):
        fine = {x: fn[f, slot(x), :] for x in range(LX)}
        fine[-2], fine[8], fine[10] = rx_lo[f, slot(0), :], rx_hi[f, slot(0), :], rx_hi[f, slot(1), :]
        coarse = {x: fy[f, slot(x), :] for x in (0, 2, 4, 6)}
        mixed = rx_hi[f, slot(2), :]
        coarse[-4], coarse[8], coarse[12] = rx_lo[f, slot(1), :], mixed, pltpu.roll(mixed, 7, 0)
        for x in range(LX):
            if x % 2 == 1:
                coef[f, x] = fine[x] - predicted(fine[x - 1], fine[x + 1], fine[x - 3], fine[x + 3])
                continue
            value = coarse[x]
            if x % 4 == 2:
                value = value - predicted(coarse[x - 2], coarse[x + 2], coarse[x - 6], coarse[x + 6])
            coef[f, x] = jnp.where(even, value, fine[x])
    store_coef = pltpu.make_async_copy(coef, o_coef, local_sem.at[4])
    store_coef.start()

    for copy in halos + lifts[0] + lifts[1] + x_copies:
        copy.wait_send()
    for i in range(3):
        max_sent(i)
    store_state.wait()
    store_reg.wait()
    store_coef.wait()


def solution(mesh):
    sizes = (mesh.shape["gx"], mesh.shape["gy"], mesh.shape["gz"])
    spec = P(None, "gx", "gy", "gz")
    any_space = pl.BlockSpec(memory_space=pl.ANY)

    def vmem(*shape):
        return pltpu.VMEM(shape, F32)

    plane = (8, LZ)
    total = sizes[0] // 2 + sizes[1] + 2 * sizes[2]
    scratch = [
        vmem(NF, LX, *plane),
        vmem(NF, LX, *plane),
        vmem(NF, SPARE + 8, LZ),
        vmem(NF, SPARE, LZ),
        vmem(NF, *plane),
        vmem(NF, *plane),
        vmem(NF, *plane),
        vmem(NF, (LX + 2) * 8, LZ),
        vmem(NF, (LX + 2) * 8, LZ),
        vmem(NF, (LX + 1) * 8, LZ),
        vmem(NF, LX, *plane),
        vmem(NF, LX, *plane),
        vmem(2, NF, 64, LZ),
        vmem(2, NF, 64, LZ),
        vmem(2, NF, 40, LZ),
        vmem(2, NF, 64, LZ),
        vmem(2, 16, LZ),
        vmem(2, 24, LZ),
        vmem(2, 16, LZ),
        vmem(2, 24, LZ),
        vmem(2, NF, 16, LZ),
        vmem(2, NF, 16, LZ),
        vmem(2, NF, 16, LZ),
        vmem(2, 64, LZ),
        vmem(2, 64, LZ),
        vmem(2, 16, LZ),
        vmem(2, LX, *plane),
        vmem(sizes[0] // 2, 1, LZ),
        vmem(sizes[1], 1, LZ),
        vmem(2 * sizes[2], 1, LZ),
        pltpu.SemaphoreType.DMA((5,)),
        pltpu.SemaphoreType.DMA((6,)),
        pltpu.SemaphoreType.DMA((6,)),
        pltpu.SemaphoreType.DMA((total,)),
        pltpu.SemaphoreType.DMA((total,)),
        pltpu.SemaphoreType.DMA((10,)),
        pltpu.SemaphoreType.DMA((10,)),
    ]

    def local(state, register):
        block = jax.ShapeDtypeStruct(state.shape, F32)
        return pl.pallas_call(
            functools.partial(kernel, sizes),
            out_shape=(block, block, jax.ShapeDtypeStruct((2,) + state.shape[1:], F32)),
            in_specs=[any_space] * 2,
            out_specs=(any_space,) * 3,
            scratch_shapes=scratch,
            compiler_params=pltpu.CompilerParams(collective_id=0, has_side_effects=True),
        )(state, register)

    return jax.shard_map(local, mesh=mesh, in_specs=(spec, spec), out_specs=(spec,) * 3, check_vma=False)
```

time: 56.3 us -> 48.2 us (0.86)
  Pallas kernels: 51.7 us -> 44.2 us
  local copies, waits for them, and re-layouts: 3.79 us -> 3.13 us
    pallas_call x1, Pallas kernels: 51.7 us -> 44.2 us  [local(): pl.pallas_call(functools.partial(kernel, sizes), out_shape=(block, block,...]
    unnamed x7, local copies, waits for them, and re-layouts: 3.79 us -> 3.13 us
where the time goes in v2:
time: 48.2 us; the launch traced here: 48 us
  Pallas kernels  44.2 us (92%)
  local copies, waits for them, and re-layouts  3.13 us (6%)
  between operations  0.65 us (1%)
    pallas_call x1, Pallas kernels, local(): pl.pallas_call(functools.partial(kernel, sizes), out_shape=(block, block,...  44.2 us
    unnamed x7, local copies, waits for them, and re-layouts  3.13 us

profile of v2, /device:TPU:1, one launch (start us, length us, event | category | flops | bytes accessed | tf_op | source)
XLA Modules:
  0.0 48.0 jit_solution(6476206817748663251)
XLA Ops:
  0.6 44.2 %shard_map.49 = (f32[5,8,8,128]{3,2,1,0:T(8,128)}, f32[5,8,8,128]{3,2,1,0:T(8,128)}, f32[2,8,8,128]{3,2,1,0:T(8,128)}) custom-call(f32[5,8,8,128]{3,2,1,0:T(8,128)} %state.1, f32[5,8,8,128]{3,2,1,0:T(8,128)} %register.1), custom_call_target="tpu_custom_call" | custom-call | tf_op jit(solution)/shard_map/pallas_call | solution.py:617
  44.9 0.0 copy-start
  44.9 1.6 %copy.8 = f32[5,8,8,128]{3,2,1,0:T(8,128)} copy(f32[5,8,8,128]{3,2,1,0:T(8,128)} %get-tuple-element.6) | data formatting | bytes 327680
  46.5 0.0 copy-done
  46.5 0.0 copy-start.1
  46.5 0.7 %copy.9 = f32[5,8,8,128]{3,2,1,0:T(8,128)} copy(f32[5,8,8,128]{3,2,1,0:T(8,128)S(1)} %copy-done) | data formatting | bytes 327680
  47.2 0.2 copy-done.1
  47.4 0.6 %copy.10 = f32[2,8,8,128]{3,2,1,0:T(8,128)} copy(f32[2,8,8,128]{3,2,1,0:T(8,128)S(1)} %copy-done.1) | data formatting | bytes 131072
Async XLA Ops:
  44.9 1.6 %copy-start = (f32[5,8,8,128]{3,2,1,0:T(8,128)S(1)}, f32[5,8,8,128]{3,2,1,0:T(8,128)}, u32[]{:S(2)}) copy-start(f32[5,8,8,128]{3,2,1,0:T(8,128)} %get-tuple-element.7) | copy-start | bytes 491524
  46.5 0.9 %copy-start.1 = (f32[2,8,8,128]{3,2,1,0:T(8,128)S(1)}, f32[2,8,8,128]{3,2,1,0:T(8,128)}, u32[]{:S(2)}) copy-start(f32[2,8,8,128]{3,2,1,0:T(8,128)} %get-tuple-element.8) | copy-start | bytes 196612

commit v3 on v2

--- a/solution.py
+++ b/solution.py
@@ -95,13 +95,13 @@
     ez,
     ezl,
     ezh,
-    ch_x,
     ch_y,
     fz,
     sn,
     rn,
-    en,
-    ey,
+    base,
+    rate,
+    ends,
     turned,
     around,
     sx_hi,
@@ -109,8 +109,7 @@
     rx_lo,
     rx_hi,
     sz,
-    rz_lo,
-    rz_hi,
+    rz,
     fn,
     fy,
     fc,
@@ -131,26 +130,36 @@
     iy = lax.axis_index("gy")
     iz = lax.axis_index("gz")
 
+    def turned_by(i, k, n):
+        k = k % n
+        return i if k == 0 else jnp.where(i >= n - k, i - (n - k), i + k)
+
     def at(dx=0, dy=0, dz=0):
-        return {
-            "gx": lax.rem(ix + (dx + nx), nx),
-            "gy": lax.rem(iy + (dy + ny), ny),
-            "gz": lax.rem(iz + (dz + nz), nz),
-        }
+        return {"gx": turned_by(ix, dx, nx), "gy": turned_by(iy, dy, ny), "gz": turned_by(iz, dz, nz)}
 
     chips_z, half_y = nx // 2, ny // 2
+    upper_half = jnp.where(ix >= chips_z, 1, 0)
+    chip_z = ix - upper_half * chips_z
+    core = lax.rem(iy, 2)
+    chip_y = upper_half * half_y + lax.div(iy, 2)
 
     def plane_mate(k):
-        return {"gx": ix, "gy": iy - iy % 2 + (iy + k // nz) % 2, "gz": (iz + k % nz) % nz}
+        return {"gx": ix, "gy": iy if k < nz else iy + 1 - 2 * core, "gz": turned_by(iz, k, nz)}
 
     def column_mate(k):
-        y = (ix // chips_z * half_y + iy // 2 + k) % (2 * half_y)
-        return {"gx": y // half_y * chips_z + ix % chips_z, "gy": y % half_y * 2 + iy % 2, "gz": iz}
+        y = turned_by(chip_y, k, 2 * half_y)
+        half = jnp.where(y >= half_y, 1, 0)
+        return {"gx": half * chips_z + chip_z, "gy": (y - half * half_y) * 2 + core, "gz": iz}
 
     def depth_mate(k):
-        return {"gx": ix - ix % chips_z + (ix + k) % chips_z, "gy": iy, "gz": iz}
+        return {"gx": upper_half * chips_z + turned_by(chip_z, k, chips_z), "gy": iy, "gz": iz}
 
     groups = ((plane_mate, 2 * nz), (column_mate, 2 * half_y), (depth_mate, chips_z))
+
+    def far_first(count):
+        return sorted(range(1, count), key=lambda k: -min(k, count - k))
+
+    orders = (sorted(range(1, 2 * nz), key=lambda k: -min(k % nz, nz - k % nz)), far_first(2 * half_y), far_first(chips_z))
 
     barrier = pltpu.get_barrier_semaphore()
 
@@ -161,16 +170,16 @@
     load_reg = pltpu.make_async_copy(register, rg, local_sem.at[1])
     load_state.start()
     load_reg.start()
-    for mate, count in groups:
-
-        def greet_mate(k, _, mate=mate):
+    for (mate, _), order in zip(groups, orders):
+        for k in order:
             greet(mate(k))
-            return 0
-
-        lax.fori_loop(1, count, greet_mate, 0)
-    for target in (at(dx=-1), at(dx=1), at(dy=-1), at(dy=1), at(dz=-1), at(dz=1)):
+    for target in (at(dx=-1), at(dx=1)):
         greet(target)
-    partners = sum(count - 1 for _, count in groups) + 6
+    for dy in (-1, 0, 1):
+        for dz in (-1, 0, 1):
+            if (dy, dz) != (0, 0):
+                greet(at(dy=dy, dz=dz))
+    partners = sum(count - 1 for _, count in groups) + 10
 
     lane = lax.broadcasted_iota(jnp.int32, (8, LZ), 1)
     row = lax.broadcasted_iota(jnp.int32, (8, LZ), 0)
@@ -214,29 +223,23 @@
     slots = (mz, my, mx)
 
     def max_copy(i, k):
-        base = bases[i]
-        return remote(slots[i].at[0], slots[i].at[k], max_send.at[base + k], max_recv.at[base + k], groups[i][0](k))
+        sem = bases[i] + k
+        return remote(slots[i].at[0], slots[i].at[k], max_send.at[sem], max_recv.at[sem], groups[i][0](k))
 
     def max_start(i):
-        def body(k, _):
+        for k in orders[i]:
             max_copy(i, k).start()
-            return 0
-
-        lax.fori_loop(1, groups[i][1], body, 0)
 
     def max_wait(i):
-        def body(k, best):
+        best = slots[i][0]
+        for k in reversed(orders[i]):
             max_copy(i, k).wait_recv()
-            return jnp.maximum(best, slots[i][k])
-
-        return lax.fori_loop(1, groups[i][1], body, slots[i][0])
+            best = jnp.maximum(best, slots[i][k])
+        return best
 
     def max_sent(i):
-        def body(k, _):
+        for k in orders[i]:
             max_copy(i, k).wait_send()
-            return 0
-
-        lax.fori_loop(1, groups[i][1], body, 0)
 
     max_start(0)
 
@@ -278,59 +281,71 @@
     def slot(i):
         return pl.ds(8 * i if isinstance(i, int) else pl.multiple_of(i * 8, 8), 8)
 
+    def plane(v, k, x):
+        if v == 0:
+            return base[k, slot(x), :]
+        return rate[k, slot(x + 2), :]
+
     def lift_copies(v):
         def one(i, src, dst, target):
-            return remote(src, dst, lift_send.at[4 * v + i], lift_recv.at[4 * v + i], target)
+            return remote(src, dst, lift_send.at[8 * v + i], lift_recv.at[8 * v + i], target)
 
         to_hi, to_lo = pl.ds(0, 16), pl.ds(16, 24)
-        return [
+        copies = [
             one(0, turned.at[v, :, to_hi, :], around.at[v, :, to_hi, :], at(dy=1)),
             one(1, turned.at[v, :, to_lo, :], around.at[v, :, to_lo, :], at(dy=-1)),
-            one(2, sz.at[v], rz_lo.at[v], at(dz=1)),
-            one(3, sz.at[v], rz_hi.at[v], at(dz=-1)),
         ]
+        for i, (dy, dz) in enumerate(((1, 1), (1, -1), (-1, 1), (-1, -1), (0, 1), (0, -1))):
+            copies.append(one(2 + i, sz.at[v], rz.at[v, i], at(dy=dy, dz=dz)))
+        return copies
 
     lifts = [lift_copies(0), lift_copies(1)]
     for v in range(2):
         for k in range(NF):
             around[v, k, pl.ds(40, 24), :] = jnp.zeros((24, LZ), F32)
 
-    def send_rows(v):
+    def send_lift(v):
+        source, first_row = ((base, 0), (rate, 16))[v]
         for k in range(NF):
             for i, y in enumerate((4, 6, 0, 2, 4)):
-                turned[v, k, pl.ds(8 * i, 8), :] = en[v, k, pl.ds(y, 8, stride=8), :]
+                turned[v, k, pl.ds(8 * i, 8), :] = source[k, pl.ds(first_row + y, 8, stride=8), :]
         lifts[v][0].start()
         lifts[v][1].start()
 
-    def send_ends(v):
-        lifts[v][0].wait_recv()
-        lifts[v][1].wait_recv()
-
         def pack_ends(x, packed):
-            out = []
-            for k in range(NF):
-                outer = around[v, k, pl.ds(x, 8, stride=8), :]
-                ey[v, k, slot(x), :] = outer
-                for j, value in enumerate((en[v, k, slot(x), :], outer)):
-                    out.append(jnp.where(group == x, pltpu.roll(value, 16 * x + 4, 1), packed[2 * k + j]))
-            return tuple(out)
-
-        packed = lax.fori_loop(0, LX, pack_ends, (zero,) * (2 * NF))
-        for k in range(NF):
-            sz[v, k, pl.ds(0, 8), :] = packed[2 * k]
-            sz[v, k, pl.ds(8, 8), :] = packed[2 * k + 1]
-        lifts[v][2].start()
-        lifts[v][3].start()
+            return tuple(
+                jnp.where(group == x, pltpu.roll(plane(v, k, x), 16 * x + 4, 1), packed[k]) for k in range(NF)
+            )
+
+        packed = lax.fori_loop(0, LX, pack_ends, (zero,) * NF)
+        for k in range(NF):
+            sz[v, k] = packed[k]
+        for copy in lifts[v][2:]:
+            copy.start()
+
+    from_low = inner < 4
+
+    def receive_lift(v):
+        for copy in lifts[v]:
+            copy.wait_recv()
+        for k in range(NF):
+            below = jnp.where(from_low, rz[v, 0, k], rz[v, 1, k])
+            above = jnp.where(from_low, rz[v, 2, k], rz[v, 3, k])
+            outer = jnp.where(row == 0, pltpu.roll(below, 4, 0), pltpu.roll(below, 3, 0))
+            outer = jnp.where(row == 2, pltpu.roll(above, 2, 0), outer)
+            outer = jnp.where(row == 3, pltpu.roll(above, 1, 0), outer)
+            ends[v, k, pl.ds(0, 8), :] = jnp.where(from_low, rz[v, 4, k], rz[v, 5, k])
+            ends[v, k, pl.ds(8, 8), :] = jnp.where(row == 4, above, outer)
 
     load_reg.wait()
 
     def make_base(x, _):
         for k in range(NF):
-            en[0, k, slot(x), :] = st[k, x] + (SECTION_GAIN * SECTION_DECAY) * rg[k, x]
+            base[k, slot(x), :] = st[k, x] + (SECTION_GAIN * SECTION_DECAY) * rg[k, x]
         return 0
 
     lax.fori_loop(0, LX, make_base, 0)
-    send_rows(0)
+    send_lift(0)
 
     my[0] = max_wait(0)
     max_start(1)
@@ -366,10 +381,10 @@
 
     lax.fori_loop(0, LX + 1, z_faces, 0)
     for k in range(NF):
-        ends = fz[k, pl.ds(64, 8), :]
-        fz[k, pl.ds(64, 8), :] = jnp.where(inner == 11, pltpu.roll(ends, 9, 1), ends)
-
-    def sweep(padded, change, normal):
+        tail = fz[k, pl.ds(64, 8), :]
+        fz[k, pl.ds(64, 8), :] = jnp.where(inner == 11, pltpu.roll(tail, 9, 1), tail)
+
+    def sweep(padded, change, normal, subtract):
         def body(j, carry):
             before, flux_before = carry
             left, right = [], []
@@ -388,7 +403,8 @@
             flux = hlle(floored(before, *sides), floored(right, *sides), normal)
             out = pl.ds(pl.multiple_of(j * 8, 8), 8)
             for k in range(NF):
-                change[k, out, :] = flux[k] - flux_before[k]
+                difference = flux[k] - flux_before[k]
+                change[k, out, :] = change[k, out, :] - difference if subtract else difference
             return tuple(left), flux
 
         one = jnp.ones((8, LZ), F32)
@@ -396,32 +412,28 @@
 
     halos[2].wait_recv()
     halos[3].wait_recv()
-    sweep(py, ch_y, 2)
-    send_ends(0)
+    sweep(py, ch_y, 2, False)
     mx[0] = max_wait(1)
     max_start(2)
+
+    def make_rate(x, _):
+        for k in range(NF):
+            faces = fz[k, slot(x), :]
+            tips = pltpu.roll(fz[k, pl.ds(64, 8), :], 117 - 16 * x, 1)
+            upper = jnp.where(lane == LZ - 1, tips, faces)
+            lower = jnp.where(lane == 0, tips, pltpu.roll(faces, 1, 1))
+            rate[k, slot(x + 2), :] = (lower - upper) - ch_y[k, pl.ds(16 + x, 8, stride=8), :]
+        return 0
+
+    lax.fori_loop(0, LX, make_rate, 0)
+    for k in range(NF):
+        rate[k, pl.ds(0, 16), :] = jnp.zeros((16, LZ), F32)
     halos[4].wait_recv()
     halos[5].wait_recv()
-    sweep(px, ch_x, 1)
-
-    def make_rate(x, _):
-        rows_x = slot(x + 2)
-        rows_z = slot(x)
-        for k in range(NF):
-            faces = fz[k, rows_z, :]
-            ends = pltpu.roll(fz[k, pl.ds(64, 8), :], 117 - 16 * x, 1)
-            upper = jnp.where(lane == LZ - 1, ends, faces)
-            lower = jnp.where(lane == 0, ends, pltpu.roll(faces, 1, 1))
-            change = ch_x[k, rows_x, :] + ch_y[k, pl.ds(16 + x, 8, stride=8), :]
-            en[1, k, rows_z, :] = -(change + (upper - lower))
-        return 0
-
-    lax.fori_loop(0, LX, make_rate, 0)
-    send_rows(1)
-    send_ends(1)
-    for v in range(2):
-        lifts[v][2].wait_recv()
-        lifts[v][3].wait_recv()
+    sweep(px, rate, 1, True)
+    send_lift(1)
+    receive_lift(0)
+    receive_lift(1)
 
     fastest = max_wait(2)
     step = jnp.broadcast_to(CFL_NUMBER / fastest, (8, LZ))
@@ -431,19 +443,18 @@
         square = new[1] * new[1] + new[2] * new[2] + new[3] * new[3]
         return 0.4 * (new[4] - 0.5 * square / new[0])
 
-    from_low = inner < 4
     for j in range(2):
-        rows = pl.ds(8 * j, 8)
-        new = []
-        for k in range(NF):
-            base = jnp.where(from_low, rz_lo[0, k, rows, :], rz_hi[0, k, rows, :])
-            rate = jnp.where(from_low, rz_lo[1, k, rows, :], rz_hi[1, k, rows, :])
-            new.append(base + gain * rate)
-        fc[0, rows, :] = pressure(new)
-        fc[1, rows, :] = new[0]
-
-    def after(ref, x):
-        new = [ref[0, k, slot(x), :] + gain * ref[1, k, slot(x), :] for k in range(NF)]
+        new = [ends[0, k, slot(j), :] + gain * ends[1, k, slot(j), :] for k in range(NF)]
+        fc[0, slot(j), :] = pressure(new)
+        fc[1, slot(j), :] = new[0]
+
+    def after(x):
+        new = [plane(0, k, x) + gain * plane(1, k, x) for k in range(NF)]
+        return pressure(new), new[0]
+
+    def after_around(x):
+        rows = pl.ds(x, 8, stride=8)
+        new = [around[0, k, rows, :] + gain * around[1, k, rows, :] for k in range(NF)]
         return pressure(new), new[0]
 
     odd_lane = lane % 2 == 1
@@ -487,13 +498,13 @@
 
     def lift_zy(x, both):
         shift = lax.rem(252 - 16 * x, LZ)
-        cells, outer = after(en, x), after(ey, x)
+        cells, outer = after(x), after_around(x)
         for f in range(2):
-            ends = pltpu.roll(fc[f, pl.ds(0, 8), :], shift, 1)
-            ends_outer = pltpu.roll(fc[f, pl.ds(8, 8), :], shift, 1)
-            fn[f, slot(x), :] = fine_y(fine_z(cells[f], ends), fine_z(outer[f], ends_outer))
+            tips = pltpu.roll(fc[f, pl.ds(0, 8), :], shift, 1)
+            tips_outer = pltpu.roll(fc[f, pl.ds(8, 8), :], shift, 1)
+            fn[f, slot(x), :] = fine_y(fine_z(cells[f], tips), fine_z(outer[f], tips_outer))
             if both:
-                fy[f, slot(x), :] = coarse_y(coarse_z(cells[f], ends), coarse_z(outer[f], ends_outer))
+                fy[f, slot(x), :] = coarse_y(coarse_z(cells[f], tips), coarse_z(outer[f], tips_outer))
 
     def lift_even(i, _):
         lift_zy(2 * i, True)
@@ -508,15 +519,15 @@
         sx_lo[f, slot(1), :] = fn[f, slot(2), :]
         sx_lo[f, slot(2), :] = jnp.where(odd_row, pltpu.roll(fy[f, slot(4), :], 1, 0), fy[f, slot(0), :])
     x_copies = [
-        remote(sx_hi, rx_lo, lift_send.at[8], lift_recv.at[8], at(dx=1)),
-        remote(sx_lo, rx_hi, lift_send.at[9], lift_recv.at[9], at(dx=-1)),
+        remote(sx_hi, rx_lo, lift_send.at[16], lift_recv.at[16], at(dx=1)),
+        remote(sx_lo, rx_hi, lift_send.at[17], lift_recv.at[17], at(dx=-1)),
     ]
     for copy in x_copies:
         copy.start()
 
     def update(x, _):
         for k in range(NF):
-            r = SECTION_DECAY * rg[k, x] + step * en[1, k, slot(x), :]
+            r = SECTION_DECAY * rg[k, x] + step * plane(1, k, x)
             rn[k, x] = r
             sn[k, x] = st[k, x] + SECTION_GAIN * r
         return 0
@@ -562,6 +573,19 @@
     store_coef.wait()
 
 
+def deliver(*refs):
+    sources, targets, stages, sems = refs[:3], refs[3:6], refs[6:9], refs[9]
+    loads = [pltpu.make_async_copy(sources[i], stages[i], sems.at[i]) for i in range(3)]
+    stores = [pltpu.make_async_copy(stages[i], targets[i], sems.at[3 + i]) for i in range(3)]
+    for load in loads:
+        load.start()
+    for load, store in zip(loads, stores):
+        load.wait()
+        store.start()
+    for store in stores:
+        store.wait()
+
+
 def solution(mesh):
     sizes = (mesh.shape["gx"], mesh.shape["gy"], mesh.shape["gz"])
     spec = P(None, "gx", "gy", "gz")
@@ -581,21 +605,20 @@
         vmem(NF, *plane),
         vmem(NF, *plane),
         vmem(NF, (LX + 2) * 8, LZ),
-        vmem(NF, (LX + 2) * 8, LZ),
         vmem(NF, (LX + 1) * 8, LZ),
         vmem(NF, LX, *plane),
         vmem(NF, LX, *plane),
-        vmem(2, NF, 64, LZ),
-        vmem(2, NF, 64, LZ),
+        vmem(NF, LX * 8, LZ),
+        vmem(NF, (LX + 2) * 8, LZ),
+        vmem(2, NF, 16, LZ),
         vmem(2, NF, 40, LZ),
         vmem(2, NF, 64, LZ),
         vmem(2, 16, LZ),
         vmem(2, 24, LZ),
         vmem(2, 16, LZ),
         vmem(2, 24, LZ),
-        vmem(2, NF, 16, LZ),
-        vmem(2, NF, 16, LZ),
-        vmem(2, NF, 16, LZ),
+        vmem(2, NF, *plane),
+        vmem(2, 6, NF, *plane),
         vmem(2, 64, LZ),
         vmem(2, 64, LZ),
         vmem(2, 16, LZ),
@@ -608,19 +631,27 @@
         pltpu.SemaphoreType.DMA((6,)),
         pltpu.SemaphoreType.DMA((total,)),
         pltpu.SemaphoreType.DMA((total,)),
-        pltpu.SemaphoreType.DMA((10,)),
-        pltpu.SemaphoreType.DMA((10,)),
+        pltpu.SemaphoreType.DMA((18,)),
+        pltpu.SemaphoreType.DMA((18,)),
     ]
 
     def local(state, register):
         block = jax.ShapeDtypeStruct(state.shape, F32)
-        return pl.pallas_call(
+        shapes = (block, block, jax.ShapeDtypeStruct((2,) + state.shape[1:], F32))
+        results = pl.pallas_call(
             functools.partial(kernel, sizes),
-            out_shape=(block, block, jax.ShapeDtypeStruct((2,) + state.shape[1:], F32)),
+            out_shape=shapes,
             in_specs=[any_space] * 2,
             out_specs=(any_space,) * 3,
             scratch_shapes=scratch,
             compiler_params=pltpu.CompilerParams(collective_id=0, has_side_effects=True),
         )(state, register)
+        return pl.pallas_call(
+            deliver,
+            out_shape=shapes,
+            in_specs=[any_space] * 3,
+            out_specs=(any_space,) * 3,
+            scratch_shapes=[pltpu.VMEM(shape.shape, F32) for shape in shapes] + [pltpu.SemaphoreType.DMA((6,))],
+        )(*results)
 
     return jax.shard_map(local, mesh=mesh, in_specs=(spec, spec), out_specs=(spec,) * 3, check_vma=False)

time: 48.2 us -> 44.7 us (0.927)
  local copies, waits for them, and re-layouts: 3.13 us -> 0 us
    unnamed x7 -> x0, local copies, waits for them, and re-layouts: 3.13 us -> none
    pallas_call x1 -> x2, Pallas kernels: 44.2 us -> 43.9 us  [the longest x1 42.1 us: local(): pl.pallas_call(functools.partial(kernel, sizes), out_shape=shapes, in_spe...]
where the time goes in v3:
time: 44.7 us; the launch traced here: 44.5 us
  Pallas kernels  43.9 us (98%)
  between operations  0.64 us (1%)
    pallas_call x1, Pallas kernels, local(): pl.pallas_call(functools.partial(kernel, sizes), out_shape=shapes, in_spe...  42.1 us
    pallas_call x1, Pallas kernels, local(): pl.pallas_call(deliver, out_shape=shapes, in_specs=[any_space] * 3, out_s...  1.73 us

profile of v3, /device:TPU:1, one launch (start us, length us, event | category | flops | bytes accessed | tf_op | source)
XLA Modules:
  0.0 44.5 jit_solution(10043425443235145020)
XLA Ops:
  0.6 42.1 %shard_map.49 = (f32[5,8,8,128]{3,2,1,0:T(8,128)}, f32[5,8,8,128]{3,2,1,0:T(8,128)}, f32[2,8,8,128]{3,2,1,0:T(8,128)}) custom-call(f32[5,8,8,128]{3,2,1,0:T(8,128)} %state.1, f32[5,8,8,128]{3,2,1,0:T(8,128)} %register.1), custom_call_target="tpu_custom_call" | custom-call | tf_op jit(solution)/shard_map/pallas_call | solution.py:641
  42.8 1.7 %shard_map.50 = (f32[5,8,8,128]{3,2,1,0:T(8,128)}, f32[5,8,8,128]{3,2,1,0:T(8,128)}, f32[2,8,8,128]{3,2,1,0:T(8,128)}) custom-call(f32[5,8,8,128]{3,2,1,0:T(8,128)} %get-tuple-element.6.refs_0_, f32[5,8,8,128]{3,2,1,0:T(8,128)} %get-tuple-element.7.refs_1_, f32[2,8,8,128]{3,2,1,0:T(8,128)} %get-tuple-element.8.refs_2_), custom_call_target="tpu_custom_call" | custom-call | tf_op jit(solution)/shard_map/pallas_call | solution.py:649

commit v4 on v3

--- a/solution.py
+++ b/solution.py
@@ -95,7 +95,10 @@
     ez,
     ezl,
     ezh,
-    ch_y,
+    sides_x,
+    sides_y,
+    flux_x,
+    flux_y,
     fz,
     sn,
     rn,
@@ -170,7 +173,7 @@
     load_reg = pltpu.make_async_copy(register, rg, local_sem.at[1])
     load_state.start()
     load_reg.start()
-    for (mate, _), order in zip(groups, orders):
+    for (mate, _), order in reversed(list(zip(groups, orders))):
         for k in order:
             greet(mate(k))
     for target in (at(dx=-1), at(dx=1)):
@@ -203,7 +206,7 @@
         return jnp.maximum(top, speed)
 
     zero = jnp.zeros((8, LZ), F32)
-    top = lax.fori_loop(0, LX, make_primitives, zero)
+    top = lax.fori_loop(0, LX, make_primitives, zero, unroll=4)
     top = jnp.max(jnp.max(top, axis=0, keepdims=True), axis=1, keepdims=True)
     mz[0] = jnp.broadcast_to(top, (1, LZ))
 
@@ -262,7 +265,7 @@
             py[k, rows, :] = px[k, pl.ds(24 + y, 8, stride=8), :]
         return 0
 
-    lax.fori_loop(0, LX, turn, 0)
+    lax.fori_loop(0, LX, turn, 0, unroll=4)
     halos[2].start()
     halos[3].start()
 
@@ -272,7 +275,7 @@
             jnp.where(group == x, pltpu.roll(px[k, rows, :], 16 * x + 3, 1), edges[k]) for k in range(NF)
         )
 
-    edges = lax.fori_loop(0, LX, pack_edges, (zero,) * NF)
+    edges = lax.fori_loop(0, LX, pack_edges, (zero,) * NF, unroll=4)
     for k in range(NF):
         ez[k] = edges[k]
     halos[0].start()
@@ -282,9 +285,7 @@
         return pl.ds(8 * i if isinstance(i, int) else pl.multiple_of(i * 8, 8), 8)
 
     def plane(v, k, x):
-        if v == 0:
-            return base[k, slot(x), :]
-        return rate[k, slot(x + 2), :]
+        return (base, rate)[v][k, slot(x), :]
 
     def lift_copies(v):
         def one(i, src, dst, target):
@@ -305,10 +306,10 @@
             around[v, k, pl.ds(40, 24), :] = jnp.zeros((24, LZ), F32)
 
     def send_lift(v):
-        source, first_row = ((base, 0), (rate, 16))[v]
+        source = (base, rate)[v]
         for k in range(NF):
             for i, y in enumerate((4, 6, 0, 2, 4)):
-                turned[v, k, pl.ds(8 * i, 8), :] = source[k, pl.ds(first_row + y, 8, stride=8), :]
+                turned[v, k, pl.ds(8 * i, 8), :] = source[k, pl.ds(y, 8, stride=8), :]
         lifts[v][0].start()
         lifts[v][1].start()
 
@@ -317,7 +318,7 @@
                 jnp.where(group == x, pltpu.roll(plane(v, k, x), 16 * x + 4, 1), packed[k]) for k in range(NF)
             )
 
-        packed = lax.fori_loop(0, LX, pack_ends, (zero,) * NF)
+        packed = lax.fori_loop(0, LX, pack_ends, (zero,) * NF, unroll=4)
         for k in range(NF):
             sz[v, k] = packed[k]
         for copy in lifts[v][2:]:
@@ -337,6 +338,50 @@
             ends[v, k, pl.ds(0, 8), :] = jnp.where(from_low, rz[v, 4, k], rz[v, 5, k])
             ends[v, k, pl.ds(8, 8), :] = jnp.where(row == 4, above, outer)
 
+
+    def cell_faces(padded, sides, j):
+        for k in range(NF):
+            a, b, c, d, e = (padded[k, slot(j + i), :] for i in range(5))
+            sides[0, k, slot(j), :], sides[1, k, slot(j), :] = weno_pair(a, b, c, d, e)
+
+    def face_flux(padded, sides, flux, normal, f):
+        lower = padded[0, slot(f + 2), :], padded[4, slot(f + 2), :]
+        upper = padded[0, slot(f + 3), :], padded[4, slot(f + 3), :]
+        left = floored([sides[0, k, slot(f), :] for k in range(NF)], lower, upper)
+        right = floored([sides[1, k, slot(f + 1), :] for k in range(NF)], lower, upper)
+        for k, value in enumerate(hlle(left, right, normal)):
+            flux[k, slot(f), :] = value
+
+    def sweep_inner(padded, sides, flux, normal):
+        def cells(i, _):
+            cell_faces(padded, sides, 3 + i)
+            cell_faces(padded, sides, 5 + i)
+            return 0
+
+        def faces(i, _):
+            face_flux(padded, sides, flux, normal, 3 + i)
+            return 0
+
+        lax.fori_loop(0, 2, cells, 0)
+        lax.fori_loop(0, 3, faces, 0)
+
+    def sweep_outer(padded, sides, flux, normal):
+        def cells(i, _):
+            cell_faces(padded, sides, i)
+            cell_faces(padded, sides, 7 + i)
+            return 0
+
+        def faces(i, _):
+            face_flux(padded, sides, flux, normal, i)
+            face_flux(padded, sides, flux, normal, 6 + i)
+            return 0
+
+        lax.fori_loop(0, 3, cells, 0)
+        lax.fori_loop(0, 3, faces, 0)
+
+    my[0] = max_wait(0)
+    max_start(1)
+
     load_reg.wait()
 
     def make_base(x, _):
@@ -344,12 +389,10 @@
             base[k, slot(x), :] = st[k, x] + (SECTION_GAIN * SECTION_DECAY) * rg[k, x]
         return 0
 
-    lax.fori_loop(0, LX, make_base, 0)
+    lax.fori_loop(0, LX, make_base, 0, unroll=4)
     send_lift(0)
-
-    my[0] = max_wait(0)
-    max_start(1)
-
+    sweep_inner(px, sides_x, flux_x, 1)
+    sweep_inner(py, sides_y, flux_y, 2)
     halos[0].wait_recv()
     halos[1].wait_recv()
     for k in range(NF):
@@ -384,35 +427,9 @@
         tail = fz[k, pl.ds(64, 8), :]
         fz[k, pl.ds(64, 8), :] = jnp.where(inner == 11, pltpu.roll(tail, 9, 1), tail)
 
-    def sweep(padded, change, normal, subtract):
-        def body(j, carry):
-            before, flux_before = carry
-            left, right = [], []
-            lower, upper = [], []
-            for k in range(NF):
-                a, b, c, d, e = (
-                    padded[k, pl.ds(pl.multiple_of((j + i) * 8, 8), 8), :] for i in range(5)
-                )
-                lk, rk = weno_pair(a, b, c, d, e)
-                left.append(lk)
-                right.append(rk)
-                if k in (0, 4):
-                    lower.append(b)
-                    upper.append(c)
-            sides = tuple(lower), tuple(upper)
-            flux = hlle(floored(before, *sides), floored(right, *sides), normal)
-            out = pl.ds(pl.multiple_of(j * 8, 8), 8)
-            for k in range(NF):
-                difference = flux[k] - flux_before[k]
-                change[k, out, :] = change[k, out, :] - difference if subtract else difference
-            return tuple(left), flux
-
-        one = jnp.ones((8, LZ), F32)
-        lax.fori_loop(0, LX + 2, body, ((one,) * NF, (one,) * NF))
-
     halos[2].wait_recv()
     halos[3].wait_recv()
-    sweep(py, ch_y, 2, False)
+    sweep_outer(py, sides_y, flux_y, 2)
     mx[0] = max_wait(1)
     max_start(2)
 
@@ -422,15 +439,22 @@
             tips = pltpu.roll(fz[k, pl.ds(64, 8), :], 117 - 16 * x, 1)
             upper = jnp.where(lane == LZ - 1, tips, faces)
             lower = jnp.where(lane == 0, tips, pltpu.roll(faces, 1, 1))
-            rate[k, slot(x + 2), :] = (lower - upper) - ch_y[k, pl.ds(16 + x, 8, stride=8), :]
+            upper_y = flux_y[k, pl.ds(8 + x, 8, stride=8), :]
+            lower_y = flux_y[k, pl.ds(x, 8, stride=8), :]
+            rate[k, slot(x), :] = (lower - upper) + (lower_y - upper_y)
         return 0
 
-    lax.fori_loop(0, LX, make_rate, 0)
-    for k in range(NF):
-        rate[k, pl.ds(0, 16), :] = jnp.zeros((16, LZ), F32)
+    lax.fori_loop(0, LX, make_rate, 0, unroll=4)
     halos[4].wait_recv()
     halos[5].wait_recv()
-    sweep(px, rate, 1, True)
+    sweep_outer(px, sides_x, flux_x, 1)
+
+    def finish_rate(x, _):
+        for k in range(NF):
+            rate[k, slot(x), :] = rate[k, slot(x), :] + (flux_x[k, slot(x), :] - flux_x[k, slot(x + 1), :])
+        return 0
+
+    lax.fori_loop(0, LX, finish_rate, 0, unroll=4)
     send_lift(1)
     receive_lift(0)
     receive_lift(1)
@@ -496,34 +520,35 @@
         up6 = jnp.where(row == 2, outer, beyond)
         return jnp.where(mid_row, c - predicted(down2, up2, down6, up6), c)
 
-    def lift_zy(x, both):
-        shift = lax.rem(252 - 16 * x, LZ)
+    def lift_zy(x, out, along_z, along_y):
         cells, outer = after(x), after_around(x)
         for f in range(2):
-            tips = pltpu.roll(fc[f, pl.ds(0, 8), :], shift, 1)
-            tips_outer = pltpu.roll(fc[f, pl.ds(8, 8), :], shift, 1)
-            fn[f, slot(x), :] = fine_y(fine_z(cells[f], tips), fine_z(outer[f], tips_outer))
-            if both:
-                fy[f, slot(x), :] = coarse_y(coarse_z(cells[f], tips), coarse_z(outer[f], tips_outer))
-
-    def lift_even(i, _):
-        lift_zy(2 * i, True)
-        return 0
-
-    lax.fori_loop(0, LX // 2, lift_even, 0)
-
+            tips = pltpu.roll(fc[f, slot(0), :], (252 - 16 * x) % LZ, 1)
+            tips_outer = pltpu.roll(fc[f, slot(1), :], (252 - 16 * x) % LZ, 1)
+            out[f, slot(x), :] = along_y(along_z(cells[f], tips), along_z(outer[f], tips_outer))
+
+    def lift_fine(x):
+        lift_zy(x, fn, fine_z, fine_y)
+
+    def lift_coarse(x):
+        lift_zy(x, fy, coarse_z, coarse_y)
+
+    to_high = remote(sx_hi, rx_lo, lift_send.at[16], lift_recv.at[16], at(dx=1))
+    to_low = remote(sx_lo, rx_hi, lift_send.at[17], lift_recv.at[17], at(dx=-1))
+    lift_fine(6)
+    lift_coarse(4)
     for f in range(2):
         sx_hi[f, slot(0), :] = fn[f, slot(6), :]
         sx_hi[f, slot(1), :] = fy[f, slot(4), :]
+    to_high.start()
+    lift_fine(0)
+    lift_fine(2)
+    lift_coarse(0)
+    for f in range(2):
         sx_lo[f, slot(0), :] = fn[f, slot(0), :]
         sx_lo[f, slot(1), :] = fn[f, slot(2), :]
         sx_lo[f, slot(2), :] = jnp.where(odd_row, pltpu.roll(fy[f, slot(4), :], 1, 0), fy[f, slot(0), :])
-    x_copies = [
-        remote(sx_hi, rx_lo, lift_send.at[16], lift_recv.at[16], at(dx=1)),
-        remote(sx_lo, rx_hi, lift_send.at[17], lift_recv.at[17], at(dx=-1)),
-    ]
-    for copy in x_copies:
-        copy.start()
+    to_low.start()
 
     def update(x, _):
         for k in range(NF):
@@ -532,20 +557,23 @@
             sn[k, x] = st[k, x] + SECTION_GAIN * r
         return 0
 
-    lax.fori_loop(0, LX, update, 0)
+    lax.fori_loop(0, LX, update, 0, unroll=4)
     store_state = pltpu.make_async_copy(sn, o_state, local_sem.at[2])
     store_reg = pltpu.make_async_copy(rn, o_reg, local_sem.at[3])
     store_state.start()
     store_reg.start()
 
-    def lift_odd(i, _):
-        lift_zy(2 * i + 1, False)
-        return 0
-
-    lax.fori_loop(0, LX // 2, lift_odd, 0)
-
-    for copy in x_copies:
-        copy.wait_recv()
+    for x in (4, 1, 3, 5, 7):
+        lift_fine(x)
+    for x in (2, 6):
+        lift_coarse(x)
+    for copy in halos + lifts[0] + lifts[1]:
+        copy.wait_send()
+    for i in range(3):
+        max_sent(i)
+
+    to_high.wait_recv()
+    to_low.wait_recv()
     even = jnp.logical_and(row % 2 == 0, lane % 2 == 0)
     for f in range(2):
         fine = {x: fn[f, slot(x), :] for x in range(LX)}
@@ -564,10 +592,8 @@
     store_coef = pltpu.make_async_copy(coef, o_coef, local_sem.at[4])
     store_coef.start()
 
-    for copy in halos + lifts[0] + lifts[1] + x_copies:
-        copy.wait_send()
-    for i in range(3):
-        max_sent(i)
+    to_high.wait_send()
+    to_low.wait_send()
     store_state.wait()
     store_reg.wait()
     store_coef.wait()
@@ -604,12 +630,15 @@
         vmem(NF, *plane),
         vmem(NF, *plane),
         vmem(NF, *plane),
-        vmem(NF, (LX + 2) * 8, LZ),
+        vmem(2, NF, (LX + 2) * 8, LZ),
+        vmem(2, NF, (LX + 2) * 8, LZ),
+        vmem(NF, (LX + 1) * 8, LZ),
+        vmem(NF, (LX + 1) * 8, LZ),
         vmem(NF, (LX + 1) * 8, LZ),
         vmem(NF, LX, *plane),
         vmem(NF, LX, *plane),
         vmem(NF, LX * 8, LZ),
-        vmem(NF, (LX + 2) * 8, LZ),
+        vmem(NF, LX * 8, LZ),
         vmem(2, NF, 16, LZ),
         vmem(2, NF, 40, LZ),
         vmem(2, NF, 64, LZ),

time: 44.7 us -> 42.4 us (0.949)
  Pallas kernels: 43.9 us -> 41.5 us
    pallas_call x1, Pallas kernels: 42.1 us -> 39.7 us  [local(): pl.pallas_call(functools.partial(kernel, sizes), out_shape=shapes, in_spe...]
where the time goes in v4:
time: 42.4 us; the launch traced here: 42.1 us
  Pallas kernels  41.5 us (98%)
  between operations  0.64 us (2%)
    pallas_call x1, Pallas kernels, local(): pl.pallas_call(functools.partial(kernel, sizes), out_shape=shapes, in_spe...  39.7 us
    pallas_call x1, Pallas kernels, local(): pl.pallas_call(deliver, out_shape=shapes, in_specs=[any_space] * 3, out_s...  1.73 us

profile of v4, /device:TPU:1, one launch (start us, length us, event | category | flops | bytes accessed | tf_op | source)
XLA Modules:
  0.0 42.1 jit_solution(5801190273257849260)
XLA Ops:
  0.6 39.7 %shard_map.49 = (f32[5,8,8,128]{3,2,1,0:T(8,128)}, f32[5,8,8,128]{3,2,1,0:T(8,128)}, f32[2,8,8,128]{3,2,1,0:T(8,128)}) custom-call(f32[5,8,8,128]{3,2,1,0:T(8,128)} %state.1, f32[5,8,8,128]{3,2,1,0:T(8,128)} %register.1), custom_call_target="tpu_custom_call" | custom-call | tf_op jit(solution)/shard_map/pallas_call | solution.py:670
  40.4 1.7 %shard_map.50 = (f32[5,8,8,128]{3,2,1,0:T(8,128)}, f32[5,8,8,128]{3,2,1,0:T(8,128)}, f32[2,8,8,128]{3,2,1,0:T(8,128)}) custom-call(f32[5,8,8,128]{3,2,1,0:T(8,128)} %get-tuple-element.6.refs_0_, f32[5,8,8,128]{3,2,1,0:T(8,128)} %get-tuple-element.7.refs_1_, f32[2,8,8,128]{3,2,1,0:T(8,128)} %get-tuple-element.8.refs_2_), custom_call_target="tpu_custom_call" | custom-call | tf_op jit(solution)/shard_map/pallas_call | solution.py:678

commit v5 on v4

--- a/solution.py
+++ b/solution.py
@@ -127,6 +127,7 @@
     max_recv,
     lift_send,
     lift_recv,
+    known,
 ):
     nx, ny, nz = sizes
     ix = lax.axis_index("gx")
@@ -173,16 +174,18 @@
     load_reg = pltpu.make_async_copy(register, rg, local_sem.at[1])
     load_state.start()
     load_reg.start()
-    for (mate, _), order in reversed(list(zip(groups, orders))):
-        for k in order:
-            greet(mate(k))
+    near = ((depth_mate, chips_z), (column_mate, 2 * half_y))
+    offsets = [(mate, k) for mate, n in near for k in sorted({2 % n, 1 % n, n - 1, (n - 2) % n} - {0})]
+    offsets += [(plane_mate, k) for k in orders[0]]
+    for mate, k in offsets:
+        greet(mate(k))
     for target in (at(dx=-1), at(dx=1)):
         greet(target)
     for dy in (-1, 0, 1):
         for dz in (-1, 0, 1):
             if (dy, dz) != (0, 0):
                 greet(at(dy=dy, dz=dz))
-    partners = sum(count - 1 for _, count in groups) + 10
+    partners = len(offsets) + 10
 
     lane = lax.broadcasted_iota(jnp.int32, (8, LZ), 1)
     row = lax.broadcasted_iota(jnp.int32, (8, LZ), 0)
@@ -243,8 +246,6 @@
     def max_sent(i):
         for k in orders[i]:
             max_copy(i, k).wait_send()
-
-    max_start(0)
 
     low, high = pl.ds(0, 24), pl.ds(88, 24)
     first, last = pl.ds(24, 24), pl.ds(64, 24)
@@ -258,6 +259,20 @@
     ]
     halos[4].start()
     halos[5].start()
+    max_start(0)
+
+    def hand_on(mate, n, sem):
+        for k in (2, n - 2):
+            pl.semaphore_signal(known.at[sem], inc=1, device_id=mate(k), device_id_type=pl.DeviceIdType.MESH)
+
+    def heard(sem):
+        pl.semaphore_wait(known.at[sem], 2)
+
+    far_y, far_z, farther_z = half_y > 2, chips_z > 5, chips_z > 9
+    if far_z:
+        hand_on(depth_mate, chips_z, 1)
+    if far_y:
+        hand_on(column_mate, 2 * half_y, 0)
 
     def turn(y, _):
         rows = pl.ds(pl.multiple_of((y + 3) * 8, 8), 8)
@@ -379,7 +394,13 @@
         lax.fori_loop(0, 3, cells, 0)
         lax.fori_loop(0, 3, faces, 0)
 
+    if far_z:
+        heard(1)
+    if farther_z:
+        hand_on(depth_mate, chips_z, 2)
     my[0] = max_wait(0)
+    if far_y:
+        heard(0)
     max_start(1)
 
     load_reg.wait()
@@ -430,8 +451,6 @@
     halos[2].wait_recv()
     halos[3].wait_recv()
     sweep_outer(py, sides_y, flux_y, 2)
-    mx[0] = max_wait(1)
-    max_start(2)
 
     def make_rate(x, _):
         for k in range(NF):
@@ -456,6 +475,10 @@
 
     lax.fori_loop(0, LX, finish_rate, 0, unroll=4)
     send_lift(1)
+    mx[0] = max_wait(1)
+    if farther_z:
+        heard(2)
+    max_start(2)
     receive_lift(0)
     receive_lift(1)
 
@@ -662,6 +685,7 @@
         pltpu.SemaphoreType.DMA((total,)),
         pltpu.SemaphoreType.DMA((18,)),
         pltpu.SemaphoreType.DMA((18,)),
+        pltpu.SemaphoreType.REGULAR((3,)),
     ]
 
     def local(state, register):

time: 42.4 us -> 41.8 us (0.986)
  Pallas kernels: 41.5 us -> 41 us
    pallas_call x1, Pallas kernels: 39.7 us -> 39.3 us  [local(): pl.pallas_call(functools.partial(kernel, sizes), out_shape=shapes, in_spe...]
where the time goes in v5:
time: 41.8 us; the launch traced here: 41.6 us
  Pallas kernels  41 us (98%)
  between operations  0.64 us (2%)
    pallas_call x1, Pallas kernels, local(): pl.pallas_call(functools.partial(kernel, sizes), out_shape=shapes, in_spe...  39.3 us
    pallas_call x1, Pallas kernels, local(): pl.pallas_call(deliver, out_shape=shapes, in_specs=[any_space] * 3, out_s...  1.73 us

profile of v5, /device:TPU:1, one launch (start us, length us, event | category | flops | bytes accessed | tf_op | source)
XLA Modules:
  0.0 41.6 jit_solution(4539776650919641327)
XLA Ops:
  0.6 39.3 %shard_map.49 = (f32[5,8,8,128]{3,2,1,0:T(8,128)}, f32[5,8,8,128]{3,2,1,0:T(8,128)}, f32[2,8,8,128]{3,2,1,0:T(8,128)}) custom-call(f32[5,8,8,128]{3,2,1,0:T(8,128)} %state.1, f32[5,8,8,128]{3,2,1,0:T(8,128)} %register.1), custom_call_target="tpu_custom_call" | custom-call | tf_op jit(solution)/shard_map/pallas_call | solution.py:694
  39.9 1.7 %shard_map.50 = (f32[5,8,8,128]{3,2,1,0:T(8,128)}, f32[5,8,8,128]{3,2,1,0:T(8,128)}, f32[2,8,8,128]{3,2,1,0:T(8,128)}) custom-call(f32[5,8,8,128]{3,2,1,0:T(8,128)} %get-tuple-element.6.refs_0_, f32[5,8,8,128]{3,2,1,0:T(8,128)} %get-tuple-element.7.refs_1_, f32[2,8,8,128]{3,2,1,0:T(8,128)} %get-tuple-element.8.refs_2_), custom_call_target="tpu_custom_call" | custom-call | tf_op jit(solution)/shard_map/pallas_call | solution.py:702

commit v6 on v5

--- a/solution.py
+++ b/solution.py
@@ -318,26 +318,27 @@
     lifts = [lift_copies(0), lift_copies(1)]
     for v in range(2):
         for k in range(NF):
-            around[v, k, pl.ds(40, 24), :] = jnp.zeros((24, LZ), F32)
-
-    def send_lift(v):
+            around[v, k, pl.ds(40, 32), :] = jnp.zeros((32, LZ), F32)
+
+    def send_lift(v, make):
         source = (base, rate)[v]
+
+        def pack_ends(x, packed):
+            values = make(x)
+            for k in range(NF):
+                source[k, slot(x), :] = values[k]
+            return tuple(jnp.where(group == x, pltpu.roll(values[k], 16 * x + 4, 1), packed[k]) for k in range(NF))
+
+        packed = lax.fori_loop(0, LX, pack_ends, (zero,) * NF, unroll=4)
+        for k in range(NF):
+            sz[v, k] = packed[k]
+        for copy in lifts[v][2:]:
+            copy.start()
         for k in range(NF):
             for i, y in enumerate((4, 6, 0, 2, 4)):
                 turned[v, k, pl.ds(8 * i, 8), :] = source[k, pl.ds(y, 8, stride=8), :]
         lifts[v][0].start()
         lifts[v][1].start()
-
-        def pack_ends(x, packed):
-            return tuple(
-                jnp.where(group == x, pltpu.roll(plane(v, k, x), 16 * x + 4, 1), packed[k]) for k in range(NF)
-            )
-
-        packed = lax.fori_loop(0, LX, pack_ends, (zero,) * NF, unroll=4)
-        for k in range(NF):
-            sz[v, k] = packed[k]
-        for copy in lifts[v][2:]:
-            copy.start()
 
     from_low = inner < 4
 
@@ -405,13 +406,10 @@
 
     load_reg.wait()
 
-    def make_base(x, _):
-        for k in range(NF):
-            base[k, slot(x), :] = st[k, x] + (SECTION_GAIN * SECTION_DECAY) * rg[k, x]
-        return 0
-
-    lax.fori_loop(0, LX, make_base, 0, unroll=4)
-    send_lift(0)
+    def make_base(x):
+        return [st[k, x] + (SECTION_GAIN * SECTION_DECAY) * rg[k, x] for k in range(NF)]
+
+    send_lift(0, make_base)
     sweep_inner(px, sides_x, flux_x, 1)
     sweep_inner(py, sides_y, flux_y, 2)
     halos[0].wait_recv()
@@ -468,13 +466,10 @@
     halos[5].wait_recv()
     sweep_outer(px, sides_x, flux_x, 1)
 
-    def finish_rate(x, _):
-        for k in range(NF):
-            rate[k, slot(x), :] = rate[k, slot(x), :] + (flux_x[k, slot(x), :] - flux_x[k, slot(x + 1), :])
-        return 0
-
-    lax.fori_loop(0, LX, finish_rate, 0, unroll=4)
-    send_lift(1)
+    def finish_rate(x):
+        return [rate[k, slot(x), :] + (flux_x[k, slot(x), :] - flux_x[k, slot(x + 1), :]) for k in range(NF)]
+
+    send_lift(1, finish_rate)
     mx[0] = max_wait(1)
     if farther_z:
         heard(2)
@@ -656,15 +651,15 @@
         vmem(2, NF, (LX + 2) * 8, LZ),
         vmem(2, NF, (LX + 2) * 8, LZ),
         vmem(NF, (LX + 1) * 8, LZ),
-        vmem(NF, (LX + 1) * 8, LZ),
+        vmem(NF, (LX + 2) * 8, LZ),
         vmem(NF, (LX + 1) * 8, LZ),
         vmem(NF, LX, *plane),
         vmem(NF, LX, *plane),
-        vmem(NF, LX * 8, LZ),
-        vmem(NF, LX * 8, LZ),
+        vmem(NF, (LX + 1) * 8, LZ),
+        vmem(NF, (LX + 1) * 8, LZ),
         vmem(2, NF, 16, LZ),
         vmem(2, NF, 40, LZ),
-        vmem(2, NF, 64, LZ),
+        vmem(2, NF, 72, LZ),
         vmem(2, 16, LZ),
         vmem(2, 24, LZ),
         vmem(2, 16, LZ),

time: 41.8 us -> 41.2 us (0.986)
  Pallas kernels: 41 us -> 40.4 us
    pallas_call x1, Pallas kernels: 39.3 us -> 38.7 us  [local(): pl.pallas_call(functools.partial(kernel, sizes), out_shape=shapes, in_spe...]
where the time goes in v6:
time: 41.2 us; the launch traced here: 41.1 us
  Pallas kernels  40.4 us (98%)
  between operations  0.64 us (2%)
    pallas_call x1, Pallas kernels, local(): pl.pallas_call(functools.partial(kernel, sizes), out_shape=shapes, in_spe...  38.7 us
    pallas_call x1, Pallas kernels, local(): pl.pallas_call(deliver, out_shape=shapes, in_specs=[any_space] * 3, out_s...  1.73 us

profile of v6, /device:TPU:1, one launch (start us, length us, event | category | flops | bytes accessed | tf_op | source)
XLA Modules:
  0.0 41.1 jit_solution(16771074507294854836)
XLA Ops:
  0.6 38.7 %shard_map.49 = (f32[5,8,8,128]{3,2,1,0:T(8,128)}, f32[5,8,8,128]{3,2,1,0:T(8,128)}, f32[2,8,8,128]{3,2,1,0:T(8,128)}) custom-call(f32[5,8,8,128]{3,2,1,0:T(8,128)} %state.1, f32[5,8,8,128]{3,2,1,0:T(8,128)} %register.1), custom_call_target="tpu_custom_call" | custom-call | tf_op jit(solution)/shard_map/pallas_call | solution.py:689
  39.3 1.7 %shard_map.50 = (f32[5,8,8,128]{3,2,1,0:T(8,128)}, f32[5,8,8,128]{3,2,1,0:T(8,128)}, f32[2,8,8,128]{3,2,1,0:T(8,128)}) custom-call(f32[5,8,8,128]{3,2,1,0:T(8,128)} %get-tuple-element.6.refs_0_, f32[5,8,8,128]{3,2,1,0:T(8,128)} %get-tuple-element.7.refs_1_, f32[2,8,8,128]{3,2,1,0:T(8,128)} %get-tuple-element.8.refs_2_), custom_call_target="tpu_custom_call" | custom-call | tf_op jit(solution)/shard_map/pallas_call | solution.py:697

commit v7 on v6

--- a/solution.py
+++ b/solution.py
@@ -392,9 +392,11 @@
             face_flux(padded, sides, flux, normal, 6 + i)
             return 0
 
-        lax.fori_loop(0, 3, cells, 0)
-        lax.fori_loop(0, 3, faces, 0)
-
+        lax.fori_loop(0, 3, cells, 0, unroll=True)
+        lax.fori_loop(0, 3, faces, 0, unroll=True)
+
+    sweep_inner(px, sides_x, flux_x, 1)
+    sweep_inner(py, sides_y, flux_y, 2)
     if far_z:
         heard(1)
     if farther_z:
@@ -410,8 +412,6 @@
         return [st[k, x] + (SECTION_GAIN * SECTION_DECAY) * rg[k, x] for k in range(NF)]
 
     send_lift(0, make_base)
-    sweep_inner(px, sides_x, flux_x, 1)
-    sweep_inner(py, sides_y, flux_y, 2)
     halos[0].wait_recv()
     halos[1].wait_recv()
     for k in range(NF):

time: 41.2 us -> 41 us (level)
  no operation moved by 1% of the time
where the time goes in v7:
time: 41 us; the launch traced here: 40.8 us
  Pallas kernels  40.1 us (98%)
  between operations  0.64 us (2%)
    pallas_call x1, Pallas kernels, local(): pl.pallas_call(functools.partial(kernel, sizes), out_shape=shapes, in_spe...  38.4 us
    pallas_call x1, Pallas kernels, local(): pl.pallas_call(deliver, out_shape=shapes, in_specs=[any_space] * 3, out_s...  1.73 us

profile of v7, /device:TPU:1, one launch (start us, length us, event | category | flops | bytes accessed | tf_op | source)
XLA Modules:
  0.0 40.8 jit_solution(449407329793417416)
XLA Ops:
  0.6 38.4 %shard_map.49 = (f32[5,8,8,128]{3,2,1,0:T(8,128)}, f32[5,8,8,128]{3,2,1,0:T(8,128)}, f32[2,8,8,128]{3,2,1,0:T(8,128)}) custom-call(f32[5,8,8,128]{3,2,1,0:T(8,128)} %state.1, f32[5,8,8,128]{3,2,1,0:T(8,128)} %register.1), custom_call_target="tpu_custom_call" | custom-call | tf_op jit(solution)/shard_map/pallas_call | solution.py:689
  39.1 1.7 %shard_map.50 = (f32[5,8,8,128]{3,2,1,0:T(8,128)}, f32[5,8,8,128]{3,2,1,0:T(8,128)}, f32[2,8,8,128]{3,2,1,0:T(8,128)}) custom-call(f32[5,8,8,128]{3,2,1,0:T(8,128)} %get-tuple-element.6.refs_0_, f32[5,8,8,128]{3,2,1,0:T(8,128)} %get-tuple-element.7.refs_1_, f32[2,8,8,128]{3,2,1,0:T(8,128)} %get-tuple-element.8.refs_2_), custom_call_target="tpu_custom_call" | custom-call | tf_op jit(solution)/shard_map/pallas_call | solution.py:697
